TPU v7x, 32 devices: a whole 2x2x4 slice. The times are simulated.
32 devices in a mesh: groups: 2 (over x), ctx: 16 (over z, y, core).
Axes of the slice: x: 2, y: 2, z: 4, core: 2. Of those that a mesh axis runs over, the one named last changes fastest.
Arguments:
- hidden: bfloat16 [8192, 14336], P(('groups', 'ctx')), parts along dimension 0, may hold values from -6 to 6
- out_grad: bfloat16 [8192, 4096], P(('groups', 'ctx')), parts along dimension 0, may hold values from -6 to 6
- in_proj: bfloat16 [14336, 64], replicated, may hold values from -0.046875 to 0.046875
- out_proj: bfloat16 [4096, 64], replicated, may hold values from -0.09375 to 0.09375
- doc_lengths: int32 [64], P('groups'), parts along dimension 0, may hold values from 1 to 1024, 4096 in all
- doc_slot: int32 [64], P('groups'), parts along dimension 0, may hold values from 0 to 31, each once
- queries: bfloat16 [256, 4096], P('ctx'), may hold values from -0.046875 to 0.046875
Outputs:
- scores: float32 [64, 256], P(('groups', 'ctx')), parts along dimension 0
There are 2 independent parts, one for each index of `groups`. A program takes and returns all parts, laid end to end along the dimension named above; an argument that names none is the same for every part. Nothing has to cross between parts.
Inputs may be any that keep to these rules, and one draw needn't show every extreme that they name: `doc_lengths`: the lengths sum to 4096; the longest document has exactly 1024 tokens. `doc_slot`: each value names one document's output row, each once.
All inputs are finite; a program needn't handle non-finite values.
Results may differ from a plain program's by a relative error of at most 0.0003.
Values may be sent and summed in bfloat16 or wider, within the bound.
No kernel may reach another device: no remote copies, remote signals or barrier semaphores. Data moves between devices by JAX's collectives and lax.ppermute only.
A program may use at most 64 MiB of HBM per device.

v0:
```python
import jax
import jax.numpy as jnp
from jax import lax
from jax.sharding import PartitionSpec as P


def shards(hidden, out_grad, in_proj, out_proj, doc_lengths, doc_slot, queries):
    token_count = hidden.shape[0]
    doc_count = doc_slot.shape[0]
    input_low = jnp.dot(hidden, in_proj, preferred_element_type=jnp.float32)
    grad_low = jnp.dot(out_grad, out_proj, preferred_element_type=jnp.float32)
    positions = lax.axis_index("ctx") * token_count + jnp.arange(token_count, dtype=jnp.int32)
    doc_ends = jnp.cumsum(doc_lengths)
    doc_index = jnp.sum((doc_ends[None, :] <= positions[:, None]).astype(jnp.int32), axis=1)
    doc_range = jnp.arange(doc_count, dtype=jnp.int32)
    membership = doc_index[:, None] == doc_range[None, :]
    slot_of_token = jnp.sum(jnp.where(membership, doc_slot[None, :], 0), axis=1)
    selector = (doc_range[:, None] == slot_of_token[None, :]).astype(jnp.float32)
    outer_rows = (grad_low[:, :, None] * input_low[:, None, :]).reshape(token_count, -1)
    owner_grads = lax.psum_scatter(
        jnp.dot(selector, outer_rows, precision=lax.Precision.HIGHEST),
        "ctx",
        scatter_dimension=0,
        tiled=True,
    )
    return jnp.dot(
        owner_grads,
        lax.all_gather(queries, "ctx", axis=0, tiled=True).astype(jnp.float32).T,
        precision=lax.Precision.HIGHEST,
    )


def solution(mesh):
    return jax.shard_map(
        shards,
        mesh=mesh,
        in_specs=(
            P(("groups", "ctx"), None),
            P(("groups", "ctx"), None),
            P(),
            P(),
            P("groups"),
            P("groups"),
            P("ctx", None),
        ),
        out_specs=P(("groups", "ctx"), None),
        check_vma=False,
    )
```

profile of v0, /device:TPU:0, one launch (start us, length us, event | category | flops | bytes accessed | tf_op | source)
XLA Modules:
  0.0 167.0 jit_solution(12940382703059503303)
XLA Ops:
  6.5 0.0 copy-start
  6.5 0.0 all-reduce.3.cloned.1.call-start
  6.5 0.9 copy.13
  7.4 0.1 reduce-window.8
  7.5 0.1 reduce
  7.6 0.0 copy-start.1
  7.6 0.5 copy-done
  8.1 1.8 %fusion.5 = f32[256,64]{0,1:T(8,128)S(1)} fusion(bf16[256,4096]{1,0:T(8,128)(2,1)S(1)} %copy-done, bf16[4096,64]{0,1:T(8,128)(2,1)} %param.10), kind=kOutput, calls=%fused_computation.11 | convolution fusion | flops 134217728 | bytes 2686976 | tf_op jit(solution)/shard_map/dot_general | solution.py:11
  10.0 0.0 copy-done.1
  10.0 5.4 %fusion.6 = f32[256,64]{0,1:T(8,128)S(1)} fusion(bf16[256,14336]{1,0:T(8,128)(2,1)} %param.7, bf16[14336,64]{0,1:T(8,128)(2,1)S(1)} %copy-done.1), kind=kOutput, calls=%fused_computation.12 | convolution fusion | flops 469762048 | bytes 9240576 | tf_op jit(solution)/shard_map/dot_general | solution.py:10
  15.4 0.0 copy-start.2
  15.4 0.5 broadcast_multiply_fusion
  15.9 0.1 convert_reduce_fusion
  16.0 0.0 copy-done.2
  16.1 0.1 select_reduce_fusion
  16.2 0.0 copy-start.3
  16.2 3.0 %fusion.2 = f32[32,4096]{1,0:T(8,128)} fusion(f32[256,4096]{0,1:T(8,128)S(1)} %bitcast.9, s32[256]{0:T(256)S(1)} %select_reduce_fusion), kind=kOutput, calls=%fused_computation.7 | convolution fusion | flops 402661376 | bytes 4719616 | tf_op jit(solution)/shard_map/dot_general | solution.py:21
  19.1 0.0 all-reduce.3.cloned.1.call-update
  19.2 0.0 all-gather.2.cloned.1.call-start
  19.2 0.7 all-gather.2.cloned.1.call-update
  19.9 0.0 copy-done.3
  19.9 0.6 dynamic-slice
  21.2 90.9 %all-reduce.3.cloned.1.call-done = f32[32,4096]{1,0:T(8,128)} async-done(((f32[32,4096]{1,0:T(8,128)}), f32[32,4096]{1,0:T(8,128)}) %all-reduce.3.cloned.1.call-update) | async-done | bytes 524304
  112.1 44.1 %all-gather.2.cloned.1.call-done = bf16[256,4096]{1,0:T(8,128)(2,1)} async-done(((bf16[16,4096]{1,0:T(8,128)(2,1)}), bf16[256,4096]{1,0:T(8,128)(2,1)}) %all-gather.2.cloned.1.call-update) | async-done | bytes 2097168 | tf_op jit(solution)/shard_map/all_gather | solution.py:28
  156.2 4.0 %fusion = f32[2,256]{1,0:T(2,128)} fusion(bf16[256,4096]{1,0:T(8,128)(2,1)} %all-gather.2.cloned.1.call-done, f32[32,4096]{1,0:T(8,128)} %all-reduce.3.cloned.1.call-done, u32[]{:T(128)S(6)} %multiply.1), kind=kOutput, calls=%fused_computation.1 | convolution fusion | flops 25165824 | bytes 2131972 | tf_op jit(solution)/shard_map/dot_general | solution.py:26
  (1 shorter events, 0.0 us)
Async XLA Ops:
  6.5 1.6 copy-start
  6.5 105.6 %all-reduce.3.cloned.1.call-start = ((), (), s32[]{:S(2)}) async-start(), calls=%async_computation.1 | async-start | bytes 1048576
  7.6 2.4 %copy-start.1 = (bf16[14336,64]{0,1:T(8,128)(2,1)S(1)}, bf16[14336,64]{0,1:T(8,128)(2,1)}, u32[]{:S(2)}) copy-start(bf16[14336,64]{0,1:T(8,128)(2,1)} %param.9) | copy-start | bytes 5505028
  15.4 0.7 copy-start.2
  16.2 3.8 %copy-start.3 = (u32[32]{0:T(128)S(1)}, u32[32]{0:T(128)}, u32[]{:S(2)}) copy-start(u32[32]{0:T(128)} %constant.13) | copy-start | bytes 388
  19.2 137.0 %all-gather.2.cloned.1.call-start = ((), (), s32[]{:S(2)}) async-start(), calls=%async_computation | async-start | bytes 2228224 | tf_op jit(solution)/shard_map/all_gather | solution.py:28
Sparse Core Ops, SparseCore 0:
  19.3 92.7 all-reduce.2
  114.3 41.8 all-gather.1
where the time goes:
time: 167 us
  waiting for transfers between devices  136 us (81%)
  matrix products  14.2 us (9%)
  between operations  14.1 us (8%)
  local copies, waits for them, and re-layouts  2.04 us (1%)
    unnamed x3, waiting for transfers between devices  91.7 us
    all_gather x1, waiting for transfers between devices, shards(): lax.all_gather(queries, 'ctx', axis=0, tiled=True).astype(jnp.float32)  44.1 us
    dot_general x1, matrix products, shards(): input_low = jnp.dot(hidden, in_proj, preferred_element_type=jnp.float32)  5.43 us
    dot_general x1, matrix products, shards(): jnp.dot(owner_grads, lax.all_gather(queries, 'ctx', axis=0, tiled=True).a...  3.98 us
  transfers between devices with their start and end apart: 2, of which 2 were waited for; matrix products, arithmetic and copies ran while one was open for 0% of the time, Pallas kernels for 0%

commit v1 on v0

v1 whole, which is shorter than its diff:
```python
import functools

import jax
import jax.numpy as jnp
from jax import lax
from jax.experimental import pallas as pl
from jax.experimental.pallas import tpu as pltpu
from jax.sharding import PartitionSpec as P

F32, BF16 = jnp.float32, jnp.bfloat16
LANES = 128
NT = (((1,), (1,)), ((), ()))


def split2(x):
    hi = x.astype(BF16)
    return hi, (x - hi.astype(F32)).astype(BF16)


def low_kernel(
    plan, hid, og, w_in, w_out, lengths, slots, keep, send,
    hid_v, og_v, w_in_v, w_out_v, pair_hi, pair_lo, sem,
):
    bits, hop_bits, k_bit, per_dev, docs, chunk = plan
    tokens = hid.shape[0]
    rank = w_in.shape[0]
    me = lax.axis_index("ctx")

    copies = []

    def fetch(src, dst, w_src, w_dst):
        steps = []
        for c in range(0, src.shape[1], chunk):
            cols = pl.ds(c, chunk)
            pair = []
            for s, d in ((src, dst), (w_src, w_dst)):
                copy = pltpu.make_async_copy(s.at[:, cols], d.at[:, cols], sem.at[len(copies)])
                copy.start()
                copies.append(copy)
                pair.append(copy)
            steps.append((cols, pair))
        return steps

    og_steps = fetch(og, og_v, w_out, w_out_v)
    hid_steps = fetch(hid, hid_v, w_in, w_in_v)

    lane = lax.broadcasted_iota(jnp.int32, (docs, docs), 1)
    sub = lax.broadcasted_iota(jnp.int32, (docs, docs), 0)
    length = jnp.broadcast_to(lengths[...], (docs, docs)).astype(F32)
    slot = jnp.broadcast_to(slots[...], (docs, docs)).astype(F32)
    ends = jnp.sum(jnp.where(lane <= sub, length, 0.0), axis=1, keepdims=True)
    starts = jnp.sum(jnp.where(lane < sub, length, 0.0), axis=1, keepdims=True)
    slot = jnp.sum(jnp.where(lane == sub, slot, 0.0), axis=1, keepdims=True).astype(jnp.int32)
    owner = slot // per_dev
    apart = owner ^ me
    row = jnp.zeros_like(slot)
    for b in hop_bits + (k_bit,):
        row = row * 2 + ((apart >> b) & 1)
    row = (row * per_dev + (slot - owner * per_dev)).astype(F32)
    token = (me * tokens + lax.broadcasted_iota(jnp.int32, (docs, tokens), 1)).astype(F32)
    inside = (token >= starts) & (token < ends)
    token_row = jnp.sum(jnp.where(inside, row, 0.0), axis=0, keepdims=True)

    def project(steps, src, w):
        total = jnp.zeros((rank, tokens), F32)
        for cols, pair in steps:
            for copy in pair:
                copy.wait()
            total += lax.dot_general(w[:, cols], src[:, cols], NT, preferred_element_type=F32)
        return total

    grad_low = project(og_steps, og_v, w_out_v)
    input_low = project(hid_steps, hid_v, w_in_v)

    half = rank // 4
    out_r = lax.broadcasted_iota(jnp.int32, (rank, rank), 0)
    in_r = lax.broadcasted_iota(jnp.int32, (rank, rank), 1)
    odd, p = out_r // (rank // 2), out_r % (rank // 2)
    mine = (me >> k_bit) & 1
    p = (p // half ^ mine) * half + p % half
    order = (in_r == 2 * p + odd).astype(BF16)
    g_hi, g_lo = split2(grad_low)
    g_hi = jnp.dot(order, g_hi, preferred_element_type=F32).astype(BF16)
    g_lo = jnp.dot(order, g_lo, preferred_element_type=F32).astype(BF16)
    pairs = rank // 2
    pair_hi[:, :tokens], pair_hi[:, tokens:] = g_hi[:pairs], g_hi[pairs:]
    pair_lo[:, :tokens], pair_lo[:, tokens:] = g_lo[:pairs], g_lo[pairs:]

    x_hi, x_lo = split2(input_low)
    zero = jnp.zeros_like(x_hi)

    def diagonal(x):
        return jnp.concatenate(
            [jnp.concatenate([x, zero], axis=1), jnp.concatenate([zero, x], axis=1)], axis=0
        )

    right_hi = diagonal(x_hi)
    right_both = jnp.concatenate([right_hi, diagonal(x_lo)], axis=0)

    in_block = 2 * per_dev
    blocks = docs // in_block
    for block in range(blocks):
        left_hi, left_lo = [], []
        for h in range(2):
            rows = pl.ds(h * half, half)
            for s in range(in_block):
                entry = block * in_block + (s + h * per_dev) % in_block
                hit = (token_row == float(entry)).astype(F32).astype(BF16)
                hit = jnp.concatenate([hit, hit], axis=1)
                left_hi.append(pair_hi[rows, :] * hit)
                left_lo.append(pair_lo[rows, :] * hit)
        left_hi, left_lo = jnp.concatenate(left_hi, axis=0), jnp.concatenate(left_lo, axis=0)
        both = lax.dot_general(left_hi, right_both, NT, preferred_element_type=F32)
        low = lax.dot_general(left_lo, right_hi, NT, preferred_element_type=F32)
        out = both[:, :LANES] + (both[:, LANES:] + low)
        size = out.shape[0]
        if block < blocks // 2:
            keep[pl.ds(block * size, size), :] = out
        else:
            send[pl.ds((block - blocks // 2) * size, size), :] = out


def score_kernel(plan, grads_a, grads_b, q_a, q_b, keep, send, left, columns, total):
    bits, q_bits, per_dev, per_q = plan
    me = lax.axis_index("ctx")
    rows = 2 * per_dev
    tiles = q_a.shape[1] // LANES
    total[...] = grads_a[...] + grads_b[...]
    pad = jnp.zeros((rows, LANES), BF16)
    for t in range(tiles):
        g = total[pl.ds(t, rows, stride=tiles), :]
        hi = g.astype(BF16)
        mid, low = split2(g - hi.astype(F32))
        left[:, pl.ds(t * LANES, LANES)] = jnp.concatenate([hi, mid, low, pad], axis=0)
    count = q_a.shape[0]
    for part, q in enumerate((q_a, q_b)):
        out = lax.dot_general(q[...], left[...], NT, preferred_element_type=F32)
        for i in range(count // per_q):
            index = part * (count // per_q) + i
            apart = 0
            for j, b in enumerate(reversed(q_bits)):
                apart = apart | (((index >> j) & 1) << b)
            at = pl.multiple_of((me ^ apart) * per_q, per_q)
            columns[pl.ds(at, per_q), :] = out[i * per_q:(i + 1) * per_q, :]
    out = columns[...].T
    out = out[:rows] + (out[rows:2 * rows] + out[2 * rows:3 * rows])
    keep[...] = out[:per_dev]
    send[...] = out[per_dev:]


def shards(n, hidden, out_grad, in_proj, out_proj, doc_lengths, doc_slot, queries):
    bits = n.bit_length() - 1
    tokens, ff = hidden.shape
    d, rank = out_proj.shape
    docs = doc_slot.shape[0]
    per_dev = docs // n
    per_q = queries.shape[0]
    k_bit = bits - 1
    hop_bits = tuple(range(bits - 1))
    me = lax.axis_index("ctx")

    def swap(x, b):
        return lax.ppermute(x, "ctx", [(i, i ^ (1 << b)) for i in range(n)])

    depth = queries.shape[1] // 2
    mine = (me >> k_bit) & 1
    q_keep = lax.dynamic_slice_in_dim(queries, mine * depth, depth, axis=1)
    q_send = lax.dynamic_slice_in_dim(queries, (1 - mine) * depth, depth, axis=1)
    q_bits = (k_bit,)
    q_parts = (q_keep, swap(q_send, k_bit))
    for b in hop_bits[1:] + hop_bits[:1]:
        q = jnp.concatenate(q_parts, axis=0)
        q_parts = (q, swap(q, b))
        q_bits = (b,) + q_bits

    chunk = 1024
    rows = docs * rank * rank // LANES
    any_spec = pl.BlockSpec(memory_space=pl.ANY)
    vmem = pl.BlockSpec(memory_space=pltpu.VMEM)
    half_shape = jax.ShapeDtypeStruct((rows // 2, LANES), F32)
    keep, send = pl.pallas_call(
        functools.partial(low_kernel, (bits, hop_bits, k_bit, per_dev, docs, chunk)),
        out_shape=(half_shape, half_shape),
        in_specs=[any_spec] * 4 + [vmem] * 2,
        out_specs=(vmem, vmem),
        scratch_shapes=[
            pltpu.VMEM((tokens, ff), BF16),
            pltpu.VMEM((tokens, d), BF16),
            pltpu.VMEM((rank, ff), BF16),
            pltpu.VMEM((rank, d), BF16),
            pltpu.VMEM((rank // 2, 2 * tokens), BF16),
            pltpu.VMEM((rank // 2, 2 * tokens), BF16),
            pltpu.SemaphoreType.DMA((2 * (ff + d) // chunk,)),
        ],
        compiler_params=pltpu.CompilerParams(vmem_limit_bytes=32 << 20),
        cost_estimate=pl.CostEstimate(
            flops=2 * tokens * rank * (ff + d),
            bytes_accessed=2 * (tokens + rank) * (ff + d),
            transcendentals=0,
        ),
        name="low",
    )(hidden, out_grad, in_proj.T, out_proj.T, doc_lengths.reshape(1, docs), doc_slot.reshape(1, docs))

    for b in hop_bits:
        got = swap(send, b)
        size = keep.shape[0] // 2
        total = keep + got
        keep, send = total[:size], total[size:]
    got = swap(send, k_bit)

    width = n * per_q
    small = jax.ShapeDtypeStruct((per_dev, width), F32)
    keep, send = pl.pallas_call(
        functools.partial(score_kernel, (bits, q_bits, per_dev, per_q)),
        out_shape=(small, small),
        in_specs=[vmem] * 4,
        out_specs=(vmem, vmem),
        scratch_shapes=[
            pltpu.VMEM((8 * per_dev, depth), BF16),
            pltpu.VMEM((width, 8 * per_dev), F32),
            pltpu.VMEM(keep.shape, F32),
        ],
        cost_estimate=pl.CostEstimate(
            flops=2 * width * depth * 8 * per_dev,
            bytes_accessed=2 * width * depth,
            transcendentals=0,
        ),
        compiler_params=pltpu.CompilerParams(vmem_limit_bytes=32 << 20),
        name="score",
    )(keep, got, *q_parts)
    return keep + swap(send, k_bit)


def solution(mesh):
    return jax.shard_map(
        functools.partial(shards, mesh.shape["ctx"]),
        mesh=mesh,
        in_specs=(
            P(("groups", "ctx"), None),
            P(("groups", "ctx"), None),
            P(),
            P(),
            P("groups"),
            P("groups"),
            P("ctx", None),
        ),
        out_specs=P(("groups", "ctx"), None),
        check_vma=False,
    )
```

time: 167 us -> 49.2 us (0.29)
  waiting for transfers between devices: 136 us -> 18.2 us
  matrix products: 14.2 us -> 0 us
  between operations: 14.1 us -> 0.11 us
  starting transfers between devices: 0.04 us -> 10.9 us
  Pallas kernels: 0 us -> 9.51 us
  local copies, waits for them, and re-layouts: 2.04 us -> 9.43 us
    unnamed x3 -> x0, waiting for transfers between devices: 91.7 us -> none
    all_gather x1 -> x0, waiting for transfers between devices: 44.1 us -> none  [shards(): lax.all_gather(queries, 'ctx', axis=0, tiled=True).astype(jnp.float32)]
    ppermute x0 -> x9, waiting for transfers between devices: none -> 18.2 us  [swap(): return lax.ppermute(x, 'ctx', [(i, i ^ 1 << b) for i in range(n)])]
    dot_general x4 -> x0, matrix products: 14.2 us -> none  [the longest x1 5.43 us: shards(): input_low = jnp.dot(hidden, in_proj, preferred_element_type=jnp.float32)]
    ppermute x0 -> x9, starting transfers between devices: none -> 10.9 us  [swap(): return lax.ppermute(x, 'ctx', [(i, i ^ 1 << b) for i in range(n)])]
    pallas_call x0 -> x2, Pallas kernels: none -> 9.51 us  [the longest x1 9 us: shards(): pl.pallas_call(functools.partial(low_kernel, (bits, hop_bits, k_bit, per_...]
    unnamed x9 -> x12, local copies, waits for them, and re-layouts: 1.16 us -> 8.52 us
  transfers between devices with their start and end apart: 2 -> 9, of which waited for: 2 -> 6; matrix products, arithmetic and copies ran while one was open for 0% -> 0% of each run, Pallas kernels for 0% -> 18%
where the time goes in v1:
time: 49.2 us; the launch traced here: 48.9 us
  waiting for transfers between devices  18.2 us (37%)
  starting transfers between devices  10.9 us (22%)
  Pallas kernels  9.51 us (19%)
  local copies, waits for them, and re-layouts  9.43 us (19%)
  other arithmetic  0.7 us (1%)
    ppermute x9, waiting for transfers between devices, swap(): return lax.ppermute(x, 'ctx', [(i, i ^ 1 << b) for i in range(n)])  18.2 us
    ppermute x9, starting transfers between devices, swap(): return lax.ppermute(x, 'ctx', [(i, i ^ 1 << b) for i in range(n)])  10.9 us
    pallas_call x1, Pallas kernels, shards(): pl.pallas_call(functools.partial(low_kernel, (bits, hop_bits, k_bit, per_...  9 us
    unnamed x12, local copies, waits for them, and re-layouts  8.52 us
  transfers between devices with their start and end apart: 9, of which 6 were waited for; matrix products, arithmetic and copies ran while one was open for 0% of the time, Pallas kernels for 18%

profile of v1, /device:TPU:0, one launch (start us, length us, event | category | flops | bytes accessed | tf_op | source)
XLA Modules:
  0.0 48.9 jit_solution(4075584910733125014)
XLA Ops:
  0.0 0.9 %constant_dynamic-slice_fusion.1 = (bf16[16,2048]{1,0:T(8,128)(2,1)S(1)}, bf16[16,2048]{1,0:T(8,128)(2,1)S(1)}) fusion(bf16[16,4096]{1,0:T(8,128)(2,1)} %param.13, s32[]{:T(128)S(6)} %select_n.6, s32[]{:T(128)S(6)} %select_n.7), kind=kLoop, calls=%fused_computation.6 | loop fusion | bytes 262152 | tf_op jit(solution)/shard_map/dynamic_slice | solution.py:167
  0.9 4.1 %collective-permute-start.4 = (bf16[16,2048]{1,0:T(8,128)(2,1)S(1)}, bf16[16,2048]{1,0:T(8,128)(2,1)S(1)}, u32[]{:S(2)}, u32[]{:S(2)}) collective-permute-start(bf16[16,2048]{1,0:T(8,128)(2,1)S(1)} %get-tuple-element.14), channel_id=1, source_target_pairs={{0,8},{1,9},{2,10},{3,11},{4,12},{5,13},{6,14},{7,15},{8,0},{9,1},... | collective-permute-start | bytes 196616 | tf_op jit(solution)/shard_map/ppermute | solution.py:163
  5.0 0.0 copy-start
  5.0 3.1 %copy-done = bf16[256,14336]{1,0:T(8,128)(2,1)S(1)} copy-done((bf16[256,14336]{1,0:T(8,128)(2,1)S(1)}, bf16[256,14336]{1,0:T(8,128)(2,1)}, u32[]{:S(2)}) %copy-start) | copy-done | bytes 7340056
  8.1 0.0 copy-start.1
  8.1 1.6 %copy-done.1 = bf16[256,4096]{1,0:T(8,128)(2,1)S(1)} copy-done((bf16[256,4096]{1,0:T(8,128)(2,1)S(1)}, bf16[256,4096]{1,0:T(8,128)(2,1)}, u32[]{:S(2)}) %copy-start.1) | copy-done | bytes 2097176
  9.7 0.0 copy-start.2
  9.7 1.5 %copy-done.2 = bf16[14336,64]{0,1:T(8,128)(2,1)S(1)} copy-done((bf16[14336,64]{0,1:T(8,128)(2,1)S(1)}, bf16[14336,64]{0,1:T(8,128)(2,1)}, u32[]{:S(2)}) %copy-start.2) | copy-done | bytes 1835032
  11.2 0.0 copy-start.3
  11.2 1.0 %copy-done.3 = bf16[4096,64]{0,1:T(8,128)(2,1)S(1)} copy-done((bf16[4096,64]{0,1:T(8,128)(2,1)S(1)}, bf16[4096,64]{0,1:T(8,128)(2,1)}, u32[]{:S(2)}) %copy-start.3) | copy-done | bytes 524312
  12.2 0.7 %copy-done.4 = s32[32]{0:T(128)S(1)} copy-done((s32[32]{0:T(128)S(1)}, s32[32]{0:T(128)}, u32[]{:S(2)}) %copy-start.4) | copy-done | bytes 152
  12.9 0.7 %copy-done.5 = s32[32]{0:T(128)S(1)} copy-done((s32[32]{0:T(128)S(1)}, s32[32]{0:T(128)}, u32[]{:S(2)}) %copy-start.5) | copy-done | bytes 152
  13.5 9.0 %low.1 = (f32[512,128]{1,0:T(8,128)S(1)}, f32[512,128]{1,0:T(8,128)S(1)}) custom-call(bf16[256,14336]{1,0:T(8,128)(2,1)S(1)} %copy-done, bf16[256,4096]{1,0:T(8,128)(2,1)S(1)} %copy-done.1, bf16[64,14336]{1,0:T(8,128)(2,1)S(1)} %bitcast.4, bf16[64,4096]{1,0:T(8,128)(2,1)S(1)} %bitcast.5, s32[1,32]{1,0:T(1,128)S(1)} %bitcast.6, s32[1,32]{1,0:T(1,128)S(1)} %bitcast.7), custom_call_target="tpu_custom_call" | custom-call | flops 603979776 | bytes 11796480 | tf_op jit(solution)/shard_map/low/pallas_call | solution.py:181
  22.5 0.1 collective-permute-start
  22.6 0.0 collective-permute-done.4
  22.6 1.6 %collective-permute-start.5 = (bf16[32,2048]{1,0:T(8,128)(2,1)S(1)}, bf16[32,2048]{1,0:T(8,128)(2,1)S(1)}, u32[]{:S(2)}, u32[]{:S(2)}) collective-permute-start(bf16[32,2048]{1,0:T(8,128)(2,1)S(1)} %pad_maximum_fusion.2), channel_id=1, source_target_pairs={{0,2},{1,3},{2,0},{3,1},{4,6},{5,7},{6,4},{7,5},{8,10},{9,11},{10,... | collective-permute-start | bytes 393224 | tf_op jit(solution)/shard_map/ppermute | solution.py:163
  24.2 0.0 collective-permute-done
  24.3 1.5 %collective-permute-start.1 = (f32[256,128]{1,0:T(8,128)S(1)}, f32[256,128]{1,0:T(8,128)S(1)}, u32[]{:S(2)}, u32[]{:S(2)}) collective-permute-start(f32[256,128]{1,0:T(8,128)S(1)} %slice.25), channel_id=1, source_target_pairs={{0,2},{1,3},{2,0},{3,1},{4,6},{5,7},{6,4},{7,5},{8,10},{9,11},{10,... | collective-permute-start | bytes 393224 | tf_op jit(solution)/shard_map/ppermute | solution.py:163
  25.8 3.2 %collective-permute-done.5 = bf16[32,2048]{1,0:T(8,128)(2,1)S(1)} collective-permute-done((bf16[32,2048]{1,0:T(8,128)(2,1)S(1)}, bf16[32,2048]{1,0:T(8,128)(2,1)S(1)}, u32[]{:S(2)}, u32[]{:S(2)}) %collective-permute-start.5) | collective-permute-done | bytes 131104 | tf_op jit(solution)/shard_map/ppermute | solution.py:163
  29.0 1.6 %collective-permute-start.6 = (bf16[64,2048]{1,0:T(8,128)(2,1)S(1)}, bf16[64,2048]{1,0:T(8,128)(2,1)S(1)}, u32[]{:S(2)}, u32[]{:S(2)}) collective-permute-start(bf16[64,2048]{1,0:T(8,128)(2,1)S(1)} %pad_maximum_fusion.1), channel_id=1, source_target_pairs={{0,4},{1,5},{2,6},{3,7},{4,0},{5,1},{6,2},{7,3},{8,12},{9,13},{10,... | collective-permute-start | bytes 786440 | tf_op jit(solution)/shard_map/ppermute | solution.py:163
  30.7 0.7 %collective-permute-done.1 = f32[256,128]{1,0:T(8,128)S(1)} collective-permute-done((f32[256,128]{1,0:T(8,128)S(1)}, f32[256,128]{1,0:T(8,128)S(1)}, u32[]{:S(2)}, u32[]{:S(2)}) %collective-permute-start.1) | collective-permute-done | bytes 131104 | tf_op jit(solution)/shard_map/ppermute | solution.py:163
  31.4 1.6 %collective-permute-start.2 = (f32[128,128]{1,0:T(8,128)S(1)}, f32[128,128]{1,0:T(8,128)S(1)}, u32[]{:S(2)}, u32[]{:S(2)}) collective-permute-start(f32[128,128]{1,0:T(8,128)S(1)} %slice.27), channel_id=1, source_target_pairs={{0,4},{1,5},{2,6},{3,7},{4,0},{5,1},{6,2},{7,3},{8,12},{9,13},{10,... | collective-permute-start | bytes 196616 | tf_op jit(solution)/shard_map/ppermute | solution.py:163
  33.1 4.2 %collective-permute-done.6 = bf16[64,2048]{1,0:T(8,128)(2,1)S(1)} collective-permute-done((bf16[64,2048]{1,0:T(8,128)(2,1)S(1)}, bf16[64,2048]{1,0:T(8,128)(2,1)S(1)}, u32[]{:S(2)}, u32[]{:S(2)}) %collective-permute-start.6) | collective-permute-done | bytes 262176 | tf_op jit(solution)/shard_map/ppermute | solution.py:163
  37.3 0.1 collective-permute-start.7
  37.4 0.6 %collective-permute-done.2 = f32[128,128]{1,0:T(8,128)S(1)} collective-permute-done((f32[128,128]{1,0:T(8,128)S(1)}, f32[128,128]{1,0:T(8,128)S(1)}, u32[]{:S(2)}, u32[]{:S(2)}) %collective-permute-start.2) | collective-permute-done | bytes 65568 | tf_op jit(solution)/shard_map/ppermute | solution.py:163
  38.0 0.3 collective-permute-start.3
  38.3 4.9 %collective-permute-done.3.grads_b = f32[64,128]{1,0:T(8,128)S(1)} collective-permute-done((f32[64,128]{1,0:T(8,128)S(1)}, f32[64,128]{1,0:T(8,128)S(1)}, u32[]{:S(2)}, u32[]{:S(2)}) %collective-permute-start.3) | collective-permute-done | bytes 32800 | tf_op jit(solution)/shard_map/ppermute | solution.py:163
  43.2 0.0 collective-permute-done.7.q_b
  43.2 0.5 %score.1 = (f32[2,256]{1,0:T(2,128)S(1)}, f32[2,256]{1,0:T(2,128)S(1)}) custom-call(f32[64,128]{1,0:T(8,128)S(1)} %get-tuple-element.16.grads_a, f32[64,128]{1,0:T(8,128)S(1)} %collective-permute-done.3.grads_b, bf16[128,2048]{1,0:T(8,128)(2,1)S(1)} %pad_maximum_fusion.q_a, bf16[128,2048]{1,0:T(8,128)(2,1)S(1)} %collective-permute-done.7.q_b), custom_call_target="tpu_custom_call" | custom-call | flops 16777216 | bytes 1048576 | tf_op jit(solution)/shard_map/score/pallas_call | solution.py:213
  43.7 0.1 collective-permute-start.8
  43.8 4.5 %collective-permute-done.8 = f32[2,256]{1,0:T(2,128)S(1)} collective-permute-done((f32[2,256]{1,0:T(2,128)S(1)}, f32[2,256]{1,0:T(2,128)S(1)}, u32[]{:S(2)}, u32[]{:S(2)}) %collective-permute-start.8) | collective-permute-done | bytes 2080 | tf_op jit(solution)/shard_map/ppermute | solution.py:163
  48.3 0.6 %add.23 = f32[2,256]{1,0:T(2,128)} add(f32[2,256]{1,0:T(2,128)S(1)} %get-tuple-element.11, f32[2,256]{1,0:T(2,128)S(1)} %collective-permute-done.8) | non-fusion elementwise | flops 512 | bytes 6144 | tf_op jit(solution)/shard_map/add | solution.py:231
  (11 shorter events, 0.1 us)
Async XLA Ops:
  0.9 21.7 %collective-permute-start.4 = (bf16[16,2048]{1,0:T(8,128)(2,1)S(1)}, bf16[16,2048]{1,0:T(8,128)(2,1)S(1)}, u32[]{:S(2)}, u32[]{:S(2)}) collective-permute-start(bf16[16,2048]{1,0:T(8,128)(2,1)S(1)} %get-tuple-element.14), channel_id=1, source_target_pairs={{0,8},{1,9},{2,10},{3,11},{4,12},{5,13},{6,14},{7,15},{8,0},{9,1},... | collective-permute-start | bytes 196616 | tf_op jit(solution)/shard_map/ppermute | solution.py:163
  5.0 3.1 %copy-start = (bf16[256,14336]{1,0:T(8,128)(2,1)S(1)}, bf16[256,14336]{1,0:T(8,128)(2,1)}, u32[]{:S(2)}) copy-start(bf16[256,14336]{1,0:T(8,128)(2,1)} %hid.1) | copy-start | bytes 22020100
  8.1 1.6 %copy-start.1 = (bf16[256,4096]{1,0:T(8,128)(2,1)S(1)}, bf16[256,4096]{1,0:T(8,128)(2,1)}, u32[]{:S(2)}) copy-start(bf16[256,4096]{1,0:T(8,128)(2,1)} %og.1) | copy-start | bytes 6291460
  9.7 1.5 %copy-start.2 = (bf16[14336,64]{0,1:T(8,128)(2,1)S(1)}, bf16[14336,64]{0,1:T(8,128)(2,1)}, u32[]{:S(2)}) copy-start(bf16[14336,64]{0,1:T(8,128)(2,1)} %param.9) | copy-start | bytes 5505028
  11.2 1.0 %copy-start.3 = (bf16[4096,64]{0,1:T(8,128)(2,1)S(1)}, bf16[4096,64]{0,1:T(8,128)(2,1)}, u32[]{:S(2)}) copy-start(bf16[4096,64]{0,1:T(8,128)(2,1)} %param.10) | copy-start | bytes 1572868
  12.2 0.7 %copy-start.4 = (s32[32]{0:T(128)S(1)}, s32[32]{0:T(128)}, u32[]{:S(2)}) copy-start(s32[32]{0:T(128)} %param.11) | copy-start | bytes 388
  12.9 0.7 %copy-start.5 = (s32[32]{0:T(128)S(1)}, s32[32]{0:T(128)}, u32[]{:S(2)}) copy-start(s32[32]{0:T(128)} %param.12) | copy-start | bytes 388
  22.5 1.7 %collective-permute-start = (f32[512,128]{1,0:T(8,128)S(1)}, f32[512,128]{1,0:T(8,128)S(1)}, u32[]{:S(2)}, u32[]{:S(2)}) collective-permute-start(f32[512,128]{1,0:T(8,128)S(1)} %get-tuple-element.10), channel_id=1, source_target_pairs={{0,1},{1,0},{2,3},{3,2},{4,5},{5,4},{6,7},{7,6},{8,9},{9,8},{10,11... | collective-permute-start | bytes 786440 | tf_op jit(solution)/shard_map/ppermute | solution.py:163
  22.6 6.4 %collective-permute-start.5 = (bf16[32,2048]{1,0:T(8,128)(2,1)S(1)}, bf16[32,2048]{1,0:T(8,128)(2,1)S(1)}, u32[]{:S(2)}, u32[]{:S(2)}) collective-permute-start(bf16[32,2048]{1,0:T(8,128)(2,1)S(1)} %pad_maximum_fusion.2), channel_id=1, source_target_pairs={{0,2},{1,3},{2,0},{3,1},{4,6},{5,7},{6,4},{7,5},{8,10},{9,11},{10,... | collective-permute-start | bytes 393224 | tf_op jit(solution)/shard_map/ppermute | solution.py:163
  24.3 7.1 %collective-permute-start.1 = (f32[256,128]{1,0:T(8,128)S(1)}, f32[256,128]{1,0:T(8,128)S(1)}, u32[]{:S(2)}, u32[]{:S(2)}) collective-permute-start(f32[256,128]{1,0:T(8,128)S(1)} %slice.25), channel_id=1, source_target_pairs={{0,2},{1,3},{2,0},{3,1},{4,6},{5,7},{6,4},{7,5},{8,10},{9,11},{10,... | collective-permute-start | bytes 393224 | tf_op jit(solution)/shard_map/ppermute | solution.py:163
  29.0 8.3 %collective-permute-start.6 = (bf16[64,2048]{1,0:T(8,128)(2,1)S(1)}, bf16[64,2048]{1,0:T(8,128)(2,1)S(1)}, u32[]{:S(2)}, u32[]{:S(2)}) collective-permute-start(bf16[64,2048]{1,0:T(8,128)(2,1)S(1)} %pad_maximum_fusion.1), channel_id=1, source_target_pairs={{0,4},{1,5},{2,6},{3,7},{4,0},{5,1},{6,2},{7,3},{8,12},{9,13},{10,... | collective-permute-start | bytes 786440 | tf_op jit(solution)/shard_map/ppermute | solution.py:163
  31.4 6.6 %collective-permute-start.2 = (f32[128,128]{1,0:T(8,128)S(1)}, f32[128,128]{1,0:T(8,128)S(1)}, u32[]{:S(2)}, u32[]{:S(2)}) collective-permute-start(f32[128,128]{1,0:T(8,128)S(1)} %slice.27), channel_id=1, source_target_pairs={{0,4},{1,5},{2,6},{3,7},{4,0},{5,1},{6,2},{7,3},{8,12},{9,13},{10,... | collective-permute-start | bytes 196616 | tf_op jit(solution)/shard_map/ppermute | solution.py:163
  37.3 5.9 %collective-permute-start.7 = (bf16[128,2048]{1,0:T(8,128)(2,1)S(1)}, bf16[128,2048]{1,0:T(8,128)(2,1)S(1)}, u32[]{:S(2)}, u32[]{:S(2)}) collective-permute-start(bf16[128,2048]{1,0:T(8,128)(2,1)S(1)} %pad_maximum_fusion.q_a), channel_id=1, source_target_pairs={{0,1},{1,0},{2,3},{3,2},{4,5},{5,4},{6,7},{7,6},{8,9},{9,8},{10,11... | collective-permute-start | bytes 1572872 | tf_op jit(solution)/shard_map/ppermute | solution.py:163
  38.0 5.2 %collective-permute-start.3 = (f32[64,128]{1,0:T(8,128)S(1)}, f32[64,128]{1,0:T(8,128)S(1)}, u32[]{:S(2)}, u32[]{:S(2)}) collective-permute-start(f32[64,128]{1,0:T(8,128)S(1)} %get-tuple-element.15), channel_id=1, source_target_pairs={{0,8},{1,9},{2,10},{3,11},{4,12},{5,13},{6,14},{7,15},{8,0},{9,1},... | collective-permute-start | bytes 98312 | tf_op jit(solution)/shard_map/ppermute | solution.py:163
  43.7 4.5 %collective-permute-start.8 = (f32[2,256]{1,0:T(2,128)S(1)}, f32[2,256]{1,0:T(2,128)S(1)}, u32[]{:S(2)}, u32[]{:S(2)}) collective-permute-start(f32[2,256]{1,0:T(2,128)S(1)} %get-tuple-element.12), channel_id=1, source_target_pairs={{0,8},{1,9},{2,10},{3,11},{4,12},{5,13},{6,14},{7,15},{8,0},{9,1},... | collective-permute-start | bytes 6152 | tf_op jit(solution)/shard_map/ppermute | solution.py:163

commit v2 on v1

--- a/solution.py
+++ b/solution.py
@@ -18,36 +18,32 @@
 
 
 def low_kernel(
-    plan, hid, og, w_in, w_out, lengths, slots, keep, send,
-    hid_v, og_v, w_in_v, w_out_v, pair_hi, pair_lo, sem,
+    plan, hid, og, w_in, w_out, documents, keep, send,
+    hid_v, og_v, w_in_v, w_out_v, pair_hi, pair_lo, og_sem, hid_sem,
 ):
-    bits, hop_bits, k_bit, per_dev, docs, chunk = plan
+    bits, hop_bits, k_bit, per_dev, docs, og_chunk, hid_chunk = plan
     tokens = hid.shape[0]
     rank = w_in.shape[0]
     me = lax.axis_index("ctx")
 
-    copies = []
-
-    def fetch(src, dst, w_src, w_dst):
-        steps = []
-        for c in range(0, src.shape[1], chunk):
-            cols = pl.ds(c, chunk)
-            pair = []
-            for s, d in ((src, dst), (w_src, w_dst)):
-                copy = pltpu.make_async_copy(s.at[:, cols], d.at[:, cols], sem.at[len(copies)])
+    og_pairs, hid_pairs = ((og, og_v), (w_out, w_out_v)), ((hid, hid_v), (w_in, w_in_v))
+
+    def fetches(i, pairs, sems, chunk):
+        cols = pl.ds(pl.multiple_of(i * chunk, chunk), chunk)
+        return cols, [
+            pltpu.make_async_copy(src.at[:, cols], dst.at[:, cols], sems.at[j, i])
+            for j, (src, dst) in enumerate(pairs)
+        ]
+
+    for pairs, sems, chunk in ((og_pairs, og_sem, og_chunk), (hid_pairs, hid_sem, hid_chunk)):
+        for i in range(pairs[0][0].shape[1] // chunk):
+            for copy in fetches(i, pairs, sems, chunk)[1]:
                 copy.start()
-                copies.append(copy)
-                pair.append(copy)
-            steps.append((cols, pair))
-        return steps
-
-    og_steps = fetch(og, og_v, w_out, w_out_v)
-    hid_steps = fetch(hid, hid_v, w_in, w_in_v)
 
     lane = lax.broadcasted_iota(jnp.int32, (docs, docs), 1)
     sub = lax.broadcasted_iota(jnp.int32, (docs, docs), 0)
-    length = jnp.broadcast_to(lengths[...], (docs, docs)).astype(F32)
-    slot = jnp.broadcast_to(slots[...], (docs, docs)).astype(F32)
+    length = jnp.broadcast_to(documents[0:1, :], (docs, docs)).astype(F32)
+    slot = jnp.broadcast_to(documents[1:2, :], (docs, docs)).astype(F32)
     ends = jnp.sum(jnp.where(lane <= sub, length, 0.0), axis=1, keepdims=True)
     starts = jnp.sum(jnp.where(lane < sub, length, 0.0), axis=1, keepdims=True)
     slot = jnp.sum(jnp.where(lane == sub, slot, 0.0), axis=1, keepdims=True).astype(jnp.int32)
@@ -61,16 +57,21 @@
     inside = (token >= starts) & (token < ends)
     token_row = jnp.sum(jnp.where(inside, row, 0.0), axis=0, keepdims=True)
 
-    def project(steps, src, w):
-        total = jnp.zeros((rank, tokens), F32)
-        for cols, pair in steps:
-            for copy in pair:
+    def project(pairs, sems, chunk):
+        (src, values), (_, weights) = pairs
+
+        def step(i, total):
+            cols, copies = fetches(i, pairs, sems, chunk)
+            for copy in copies:
                 copy.wait()
-            total += lax.dot_general(w[:, cols], src[:, cols], NT, preferred_element_type=F32)
-        return total
-
-    grad_low = project(og_steps, og_v, w_out_v)
-    input_low = project(hid_steps, hid_v, w_in_v)
+            return total + lax.dot_general(
+                weights[:, cols], values[:, cols], NT, preferred_element_type=F32
+            )
+
+        return lax.fori_loop(0, src.shape[1] // chunk, step, jnp.zeros((rank, tokens), F32))
+
+    grad_low = project(og_pairs, og_sem, og_chunk)
+    input_low = project(hid_pairs, hid_sem, hid_chunk)
 
     half = rank // 4
     out_r = lax.broadcasted_iota(jnp.int32, (rank, rank), 0)
@@ -120,11 +121,9 @@
             send[pl.ds((block - blocks // 2) * size, size), :] = out
 
 
-def score_kernel(plan, grads_a, grads_b, q_a, q_b, keep, send, left, columns, total):
-    bits, q_bits, per_dev, per_q = plan
-    me = lax.axis_index("ctx")
+def near_kernel(per_dev, grads_a, grads_b, q, left, out, total):
     rows = 2 * per_dev
-    tiles = q_a.shape[1] // LANES
+    tiles = q.shape[1] // LANES
     total[...] = grads_a[...] + grads_b[...]
     pad = jnp.zeros((rows, LANES), BF16)
     for t in range(tiles):
@@ -132,9 +131,15 @@
         hi = g.astype(BF16)
         mid, low = split2(g - hi.astype(F32))
         left[:, pl.ds(t * LANES, LANES)] = jnp.concatenate([hi, mid, low, pad], axis=0)
-    count = q_a.shape[0]
-    for part, q in enumerate((q_a, q_b)):
-        out = lax.dot_general(q[...], left[...], NT, preferred_element_type=F32)
+    out[...] = lax.dot_general(q[...], left[...], NT, preferred_element_type=F32)
+
+
+def score_kernel(q_bits, per_dev, per_q, left, out_a, q_b, keep, send, columns):
+    me = lax.axis_index("ctx")
+    rows = 2 * per_dev
+    count = q_b.shape[0]
+    out_b = lax.dot_general(q_b[...], left[...], NT, preferred_element_type=F32)
+    for part, out in enumerate((out_a[...], out_b)):
         for i in range(count // per_q):
             index = part * (count // per_q) + i
             apart = 0
@@ -168,20 +173,20 @@
     q_send = lax.dynamic_slice_in_dim(queries, (1 - mine) * depth, depth, axis=1)
     q_bits = (k_bit,)
     q_parts = (q_keep, swap(q_send, k_bit))
-    for b in hop_bits[1:] + hop_bits[:1]:
+    for b in hop_bits[::-1]:
         q = jnp.concatenate(q_parts, axis=0)
         q_parts = (q, swap(q, b))
         q_bits = (b,) + q_bits
 
-    chunk = 1024
+    og_chunk, hid_chunk = 2048, 3584
     rows = docs * rank * rank // LANES
     any_spec = pl.BlockSpec(memory_space=pl.ANY)
     vmem = pl.BlockSpec(memory_space=pltpu.VMEM)
     half_shape = jax.ShapeDtypeStruct((rows // 2, LANES), F32)
     keep, send = pl.pallas_call(
-        functools.partial(low_kernel, (bits, hop_bits, k_bit, per_dev, docs, chunk)),
+        functools.partial(low_kernel, (bits, hop_bits, k_bit, per_dev, docs, og_chunk, hid_chunk)),
         out_shape=(half_shape, half_shape),
-        in_specs=[any_spec] * 4 + [vmem] * 2,
+        in_specs=[any_spec] * 4 + [vmem],
         out_specs=(vmem, vmem),
         scratch_shapes=[
             pltpu.VMEM((tokens, ff), BF16),
@@ -190,16 +195,17 @@
             pltpu.VMEM((rank, d), BF16),
             pltpu.VMEM((rank // 2, 2 * tokens), BF16),
             pltpu.VMEM((rank // 2, 2 * tokens), BF16),
-            pltpu.SemaphoreType.DMA((2 * (ff + d) // chunk,)),
+            pltpu.SemaphoreType.DMA((2, d // og_chunk)),
+            pltpu.SemaphoreType.DMA((2, ff // hid_chunk)),
         ],
-        compiler_params=pltpu.CompilerParams(vmem_limit_bytes=32 << 20),
+        compiler_params=pltpu.CompilerParams(vmem_limit_bytes=53 << 20),
         cost_estimate=pl.CostEstimate(
             flops=2 * tokens * rank * (ff + d),
             bytes_accessed=2 * (tokens + rank) * (ff + d),
             transcendentals=0,
         ),
         name="low",
-    )(hidden, out_grad, in_proj.T, out_proj.T, doc_lengths.reshape(1, docs), doc_slot.reshape(1, docs))
+    )(hidden, out_grad, in_proj.T, out_proj.T, jnp.stack([doc_lengths, doc_slot]))
 
     for b in hop_bits:
         got = swap(send, b)
@@ -209,25 +215,30 @@
     got = swap(send, k_bit)
 
     width = n * per_q
+    terms = 8 * per_dev
+    left, out = pl.pallas_call(
+        functools.partial(near_kernel, per_dev),
+        out_shape=(
+            jax.ShapeDtypeStruct((terms, depth), BF16),
+            jax.ShapeDtypeStruct((width // 2, terms), F32),
+        ),
+        in_specs=[vmem] * 3,
+        out_specs=(vmem, vmem),
+        scratch_shapes=[pltpu.VMEM(keep.shape, F32)],
+        compiler_params=pltpu.CompilerParams(vmem_limit_bytes=32 << 20),
+        cost_estimate=pl.CostEstimate(flops=1 << 34, bytes_accessed=1 << 26, transcendentals=0),
+        name="near_scores",
+    )(keep, got, q_parts[0])
     small = jax.ShapeDtypeStruct((per_dev, width), F32)
     keep, send = pl.pallas_call(
-        functools.partial(score_kernel, (bits, q_bits, per_dev, per_q)),
+        functools.partial(score_kernel, q_bits, per_dev, per_q),
         out_shape=(small, small),
-        in_specs=[vmem] * 4,
+        in_specs=[vmem] * 3,
         out_specs=(vmem, vmem),
-        scratch_shapes=[
-            pltpu.VMEM((8 * per_dev, depth), BF16),
-            pltpu.VMEM((width, 8 * per_dev), F32),
-            pltpu.VMEM(keep.shape, F32),
-        ],
-        cost_estimate=pl.CostEstimate(
-            flops=2 * width * depth * 8 * per_dev,
-            bytes_accessed=2 * width * depth,
-            transcendentals=0,
-        ),
+        scratch_shapes=[pltpu.VMEM((width, terms), F32)],
         compiler_params=pltpu.CompilerParams(vmem_limit_bytes=32 << 20),
-        name="score",
-    )(keep, got, *q_parts)
+        name="scores",
+    )(left, out, q_parts[1])
     return keep + swap(send, k_bit)
 
 

time: 49.2 us -> 38 us (0.77)
  local copies, waits for them, and re-layouts: 9.43 us -> 0.04 us
  waiting for transfers between devices: 18.2 us -> 11.8 us
  starting transfers between devices: 10.9 us -> 15.4 us
  other arithmetic: 0.7 us -> 1.38 us
    unnamed x12 -> x2, local copies, waits for them, and re-layouts: 8.52 us -> 0.01 us
    ppermute x9, waiting for transfers between devices: 18.2 us -> 11.8 us  [swap(): return lax.ppermute(x, 'ctx', [(i, i ^ 1 << b) for i in range(n)])]
    ppermute x9, starting transfers between devices: 10.9 us -> 15.4 us  [swap(): return lax.ppermute(x, 'ctx', [(i, i ^ 1 << b) for i in range(n)])]
    dynamic_slice x1, local copies, waits for them, and re-layouts: 0.88 us -> 0.01 us  [shards(): q_keep = lax.dynamic_slice_in_dim(queries, mine * depth, depth, axis=1)]
    another operation x0 -> x1, other arithmetic: none -> 0.68 us  [shards(): jnp.stack([doc_lengths, doc_slot])]
  transfers between devices with their start and end apart: 9 -> 9, of which waited for: 6 -> 6; matrix products, arithmetic and copies ran while one was open for 0% -> 0% of each run, Pallas kernels for 18% -> 1%
where the time goes in v2:
time: 38 us; the launch traced here: 37.9 us
  starting transfers between devices  15.4 us (41%)
  waiting for transfers between devices  11.8 us (31%)
  Pallas kernels  9.18 us (24%)
  other arithmetic  1.38 us (4%)
    ppermute x9, starting transfers between devices, swap(): return lax.ppermute(x, 'ctx', [(i, i ^ 1 << b) for i in range(n)])  15.4 us
    ppermute x9, waiting for transfers between devices, swap(): return lax.ppermute(x, 'ctx', [(i, i ^ 1 << b) for i in range(n)])  11.8 us
    pallas_call x1, Pallas kernels, shards(): pl.pallas_call(functools.partial(low_kernel, (bits, hop_bits, k_bit, per_...  8.54 us
  transfers between devices with their start and end apart: 9, of which 6 were waited for; matrix products, arithmetic and copies ran while one was open for 0% of the time, Pallas kernels for 1%

profile of v2, /device:TPU:0, one launch (start us, length us, event | category | flops | bytes accessed | tf_op | source)
XLA Modules:
  0.0 37.9 jit_solution(15428179051355360046)
XLA Ops:
  0.0 0.7 %pad_add_fusion.documents = s32[2,32]{1,0:T(2,128)S(1)} fusion(s32[1,32]{1,0:T(1,128)} %bitcast.6, s32[1,32]{1,0:T(1,128)} %bitcast.7), kind=kLoop, calls=%fused_computation.5 | loop fusion | flops 64 | bytes 512 | tf_op jit(solution)/shard_map/stack | solution.py:208
  0.7 0.0 copy-start
  0.7 8.5 %low.1 = (f32[512,128]{1,0:T(8,128)S(1)}, f32[512,128]{1,0:T(8,128)S(1)}) custom-call(bf16[256,14336]{1,0:T(8,128)(2,1)} %hid.1, bf16[256,4096]{1,0:T(8,128)(2,1)} %og.1, bf16[64,14336]{1,0:T(8,128)(2,1)} %bitcast.4, bf16[64,4096]{1,0:T(8,128)(2,1)} %bitcast.5, s32[2,32]{1,0:T(2,128)S(1)} %pad_add_fusion.documents), custom_call_target="tpu_custom_call" | custom-call | flops 603979776 | bytes 11796480 | tf_op jit(solution)/shard_map/low/pallas_call | solution.py:186
  9.2 0.5 %collective-permute-start = (f32[512,128]{1,0:T(8,128)S(1)}, f32[512,128]{1,0:T(8,128)S(1)}, u32[]{:S(2)}, u32[]{:S(2)}) collective-permute-start(f32[512,128]{1,0:T(8,128)S(1)} %get-tuple-element.12), channel_id=1, source_target_pairs={{0,1},{1,0},{2,3},{3,2},{4,5},{5,4},{6,7},{7,6},{8,9},{9,8},{10,11... | collective-permute-start | bytes 786440 | tf_op jit(solution)/shard_map/ppermute | solution.py:168
  9.7 0.0 copy-done
  9.8 3.7 %collective-permute-start.4 = (bf16[16,2048]{1,0:T(8,128)(2,1)S(1)}, bf16[16,2048]{1,0:T(8,128)(2,1)S(1)}, u32[]{:S(2)}, u32[]{:S(2)}) collective-permute-start(bf16[16,2048]{1,0:T(8,128)(2,1)S(1)} %get-tuple-element.18), channel_id=1, source_target_pairs={{0,8},{1,9},{2,10},{3,11},{4,12},{5,13},{6,14},{7,15},{8,0},{9,1},... | collective-permute-start | bytes 196616 | tf_op jit(solution)/shard_map/ppermute | solution.py:168
  13.4 0.0 collective-permute-done
  13.5 1.6 %collective-permute-start.1 = (f32[256,128]{1,0:T(8,128)S(1)}, f32[256,128]{1,0:T(8,128)S(1)}, u32[]{:S(2)}, u32[]{:S(2)}) collective-permute-start(f32[256,128]{1,0:T(8,128)S(1)} %slice.25), channel_id=1, source_target_pairs={{0,2},{1,3},{2,0},{3,1},{4,6},{5,7},{6,4},{7,5},{8,10},{9,11},{10,... | collective-permute-start | bytes 393224 | tf_op jit(solution)/shard_map/ppermute | solution.py:168
  15.1 2.5 %collective-permute-done.4 = bf16[16,2048]{1,0:T(8,128)(2,1)S(1)} collective-permute-done((bf16[16,2048]{1,0:T(8,128)(2,1)S(1)}, bf16[16,2048]{1,0:T(8,128)(2,1)S(1)}, u32[]{:S(2)}, u32[]{:S(2)}) %collective-permute-start.4) | collective-permute-done | bytes 65568 | tf_op jit(solution)/shard_map/ppermute | solution.py:168
  17.6 0.8 %collective-permute-start.5 = (bf16[32,2048]{1,0:T(8,128)(2,1)S(1)}, bf16[32,2048]{1,0:T(8,128)(2,1)S(1)}, u32[]{:S(2)}, u32[]{:S(2)}) collective-permute-start(bf16[32,2048]{1,0:T(8,128)(2,1)S(1)} %pad_maximum_fusion.2), channel_id=1, source_target_pairs={{0,4},{1,5},{2,6},{3,7},{4,0},{5,1},{6,2},{7,3},{8,12},{9,13},{10,... | collective-permute-start | bytes 393224 | tf_op jit(solution)/shard_map/ppermute | solution.py:168
  18.4 0.8 %collective-permute-done.1 = f32[256,128]{1,0:T(8,128)S(1)} collective-permute-done((f32[256,128]{1,0:T(8,128)S(1)}, f32[256,128]{1,0:T(8,128)S(1)}, u32[]{:S(2)}, u32[]{:S(2)}) %collective-permute-start.1) | collective-permute-done | bytes 131104 | tf_op jit(solution)/shard_map/ppermute | solution.py:168
  19.2 1.6 %collective-permute-start.2 = (f32[128,128]{1,0:T(8,128)S(1)}, f32[128,128]{1,0:T(8,128)S(1)}, u32[]{:S(2)}, u32[]{:S(2)}) collective-permute-start(f32[128,128]{1,0:T(8,128)S(1)} %slice.27), channel_id=1, source_target_pairs={{0,4},{1,5},{2,6},{3,7},{4,0},{5,1},{6,2},{7,3},{8,12},{9,13},{10,... | collective-permute-start | bytes 196616 | tf_op jit(solution)/shard_map/ppermute | solution.py:168
  20.8 2.8 %collective-permute-done.5 = bf16[32,2048]{1,0:T(8,128)(2,1)S(1)} collective-permute-done((bf16[32,2048]{1,0:T(8,128)(2,1)S(1)}, bf16[32,2048]{1,0:T(8,128)(2,1)S(1)}, u32[]{:S(2)}, u32[]{:S(2)}) %collective-permute-start.5) | collective-permute-done | bytes 131104 | tf_op jit(solution)/shard_map/ppermute | solution.py:168
  23.7 1.3 %collective-permute-start.6 = (bf16[64,2048]{1,0:T(8,128)(2,1)S(1)}, bf16[64,2048]{1,0:T(8,128)(2,1)S(1)}, u32[]{:S(2)}, u32[]{:S(2)}) collective-permute-start(bf16[64,2048]{1,0:T(8,128)(2,1)S(1)} %pad_maximum_fusion.1), channel_id=1, source_target_pairs={{0,2},{1,3},{2,0},{3,1},{4,6},{5,7},{6,4},{7,5},{8,10},{9,11},{10,... | collective-permute-start | bytes 786440 | tf_op jit(solution)/shard_map/ppermute | solution.py:168
  24.9 0.0 collective-permute-done.2
  25.0 2.8 %collective-permute-start.3 = (f32[64,128]{1,0:T(8,128)S(1)}, f32[64,128]{1,0:T(8,128)S(1)}, u32[]{:S(2)}, u32[]{:S(2)}) collective-permute-start(f32[64,128]{1,0:T(8,128)S(1)} %get-tuple-element.19), channel_id=1, source_target_pairs={{0,8},{1,9},{2,10},{3,11},{4,12},{5,13},{6,14},{7,15},{8,0},{9,1},... | collective-permute-start | bytes 98312 | tf_op jit(solution)/shard_map/ppermute | solution.py:168
  27.8 2.5 %collective-permute-done.6 = bf16[64,2048]{1,0:T(8,128)(2,1)S(1)} collective-permute-done((bf16[64,2048]{1,0:T(8,128)(2,1)S(1)}, bf16[64,2048]{1,0:T(8,128)(2,1)S(1)}, u32[]{:S(2)}, u32[]{:S(2)}) %collective-permute-start.6) | collective-permute-done | bytes 262176 | tf_op jit(solution)/shard_map/ppermute | solution.py:168
  30.3 0.1 collective-permute-start.7
  30.4 0.0 collective-permute-done.3.grads_b
  30.4 0.3 near_scores.1
  30.7 1.6 %collective-permute-done.7.q_b = bf16[128,2048]{1,0:T(8,128)(2,1)S(1)} collective-permute-done((bf16[128,2048]{1,0:T(8,128)(2,1)S(1)}, bf16[128,2048]{1,0:T(8,128)(2,1)S(1)}, u32[]{:S(2)}, u32[]{:S(2)}) %collective-permute-start.7) | collective-permute-done | bytes 524320 | tf_op jit(solution)/shard_map/ppermute | solution.py:168
  32.3 0.3 scores.1
  32.7 3.1 %collective-permute-start.8 = (f32[2,256]{1,0:T(2,128)S(1)}, f32[2,256]{1,0:T(2,128)S(1)}, u32[]{:S(2)}, u32[]{:S(2)}) collective-permute-start(f32[2,256]{1,0:T(2,128)S(1)} %get-tuple-element.16), channel_id=1, source_target_pairs={{0,8},{1,9},{2,10},{3,11},{4,12},{5,13},{6,14},{7,15},{8,0},{9,1},... | collective-permute-start | bytes 6152 | tf_op jit(solution)/shard_map/ppermute | solution.py:168
  35.7 1.6 %collective-permute-done.8 = f32[2,256]{1,0:T(2,128)S(1)} collective-permute-done((f32[2,256]{1,0:T(2,128)S(1)}, f32[2,256]{1,0:T(2,128)S(1)}, u32[]{:S(2)}, u32[]{:S(2)}) %collective-permute-start.8) | collective-permute-done | bytes 2080 | tf_op jit(solution)/shard_map/ppermute | solution.py:168
  37.3 0.6 %add.23 = f32[2,256]{1,0:T(2,128)} add(f32[2,256]{1,0:T(2,128)S(1)} %get-tuple-element.15, f32[2,256]{1,0:T(2,128)S(1)} %collective-permute-done.8) | non-fusion elementwise | flops 512 | bytes 6144 | tf_op jit(solution)/shard_map/add | solution.py:242
  (10 shorter events, 0.2 us)
Async XLA Ops:
  0.7 9.1 %copy-start = (bf16[16,4096]{1,0:T(8,128)(2,1)S(1)}, bf16[16,4096]{1,0:T(8,128)(2,1)}, u32[]{:S(2)}) copy-start(bf16[16,4096]{1,0:T(8,128)(2,1)} %param.13) | copy-start | bytes 393220
  9.2 4.2 %collective-permute-start = (f32[512,128]{1,0:T(8,128)S(1)}, f32[512,128]{1,0:T(8,128)S(1)}, u32[]{:S(2)}, u32[]{:S(2)}) collective-permute-start(f32[512,128]{1,0:T(8,128)S(1)} %get-tuple-element.12), channel_id=1, source_target_pairs={{0,1},{1,0},{2,3},{3,2},{4,5},{5,4},{6,7},{7,6},{8,9},{9,8},{10,11... | collective-permute-start | bytes 786440 | tf_op jit(solution)/shard_map/ppermute | solution.py:168
  9.8 7.8 %collective-permute-start.4 = (bf16[16,2048]{1,0:T(8,128)(2,1)S(1)}, bf16[16,2048]{1,0:T(8,128)(2,1)S(1)}, u32[]{:S(2)}, u32[]{:S(2)}) collective-permute-start(bf16[16,2048]{1,0:T(8,128)(2,1)S(1)} %get-tuple-element.18), channel_id=1, source_target_pairs={{0,8},{1,9},{2,10},{3,11},{4,12},{5,13},{6,14},{7,15},{8,0},{9,1},... | collective-permute-start | bytes 196616 | tf_op jit(solution)/shard_map/ppermute | solution.py:168
  13.5 5.7 %collective-permute-start.1 = (f32[256,128]{1,0:T(8,128)S(1)}, f32[256,128]{1,0:T(8,128)S(1)}, u32[]{:S(2)}, u32[]{:S(2)}) collective-permute-start(f32[256,128]{1,0:T(8,128)S(1)} %slice.25), channel_id=1, source_target_pairs={{0,2},{1,3},{2,0},{3,1},{4,6},{5,7},{6,4},{7,5},{8,10},{9,11},{10,... | collective-permute-start | bytes 393224 | tf_op jit(solution)/shard_map/ppermute | solution.py:168
  17.6 6.1 %collective-permute-start.5 = (bf16[32,2048]{1,0:T(8,128)(2,1)S(1)}, bf16[32,2048]{1,0:T(8,128)(2,1)S(1)}, u32[]{:S(2)}, u32[]{:S(2)}) collective-permute-start(bf16[32,2048]{1,0:T(8,128)(2,1)S(1)} %pad_maximum_fusion.2), channel_id=1, source_target_pairs={{0,4},{1,5},{2,6},{3,7},{4,0},{5,1},{6,2},{7,3},{8,12},{9,13},{10,... | collective-permute-start | bytes 393224 | tf_op jit(solution)/shard_map/ppermute | solution.py:168
  19.2 5.7 %collective-permute-start.2 = (f32[128,128]{1,0:T(8,128)S(1)}, f32[128,128]{1,0:T(8,128)S(1)}, u32[]{:S(2)}, u32[]{:S(2)}) collective-permute-start(f32[128,128]{1,0:T(8,128)S(1)} %slice.27), channel_id=1, source_target_pairs={{0,4},{1,5},{2,6},{3,7},{4,0},{5,1},{6,2},{7,3},{8,12},{9,13},{10,... | collective-permute-start | bytes 196616 | tf_op jit(solution)/shard_map/ppermute | solution.py:168
  23.7 6.6 %collective-permute-start.6 = (bf16[64,2048]{1,0:T(8,128)(2,1)S(1)}, bf16[64,2048]{1,0:T(8,128)(2,1)S(1)}, u32[]{:S(2)}, u32[]{:S(2)}) collective-permute-start(bf16[64,2048]{1,0:T(8,128)(2,1)S(1)} %pad_maximum_fusion.1), channel_id=1, source_target_pairs={{0,2},{1,3},{2,0},{3,1},{4,6},{5,7},{6,4},{7,5},{8,10},{9,11},{10,... | collective-permute-start | bytes 786440 | tf_op jit(solution)/shard_map/ppermute | solution.py:168
  25.0 5.5 %collective-permute-start.3 = (f32[64,128]{1,0:T(8,128)S(1)}, f32[64,128]{1,0:T(8,128)S(1)}, u32[]{:S(2)}, u32[]{:S(2)}) collective-permute-start(f32[64,128]{1,0:T(8,128)S(1)} %get-tuple-element.19), channel_id=1, source_target_pairs={{0,8},{1,9},{2,10},{3,11},{4,12},{5,13},{6,14},{7,15},{8,0},{9,1},... | collective-permute-start | bytes 98312 | tf_op jit(solution)/shard_map/ppermute | solution.py:168
  30.3 2.0 %collective-permute-start.7 = (bf16[128,2048]{1,0:T(8,128)(2,1)S(1)}, bf16[128,2048]{1,0:T(8,128)(2,1)S(1)}, u32[]{:S(2)}, u32[]{:S(2)}) collective-permute-start(bf16[128,2048]{1,0:T(8,128)(2,1)S(1)} %pad_maximum_fusion.q), channel_id=1, source_target_pairs={{0,1},{1,0},{2,3},{3,2},{4,5},{5,4},{6,7},{7,6},{8,9},{9,8},{10,11... | collective-permute-start | bytes 1572872 | tf_op jit(solution)/shard_map/ppermute | solution.py:168
  32.7 4.7 %collective-permute-start.8 = (f32[2,256]{1,0:T(2,128)S(1)}, f32[2,256]{1,0:T(2,128)S(1)}, u32[]{:S(2)}, u32[]{:S(2)}) collective-permute-start(f32[2,256]{1,0:T(2,128)S(1)} %get-tuple-element.16), channel_id=1, source_target_pairs={{0,8},{1,9},{2,10},{3,11},{4,12},{5,13},{6,14},{7,15},{8,0},{9,1},... | collective-permute-start | bytes 6152 | tf_op jit(solution)/shard_map/ppermute | solution.py:168

commit v3 on v2

--- a/solution.py
+++ b/solution.py
@@ -19,7 +19,7 @@
 
 def low_kernel(
     plan, hid, og, w_in, w_out, documents, keep, send,
-    hid_v, og_v, w_in_v, w_out_v, pair_hi, pair_lo, og_sem, hid_sem,
+    hid_v, og_v, w_in_v, w_out_v, pair_hi, pair_lo, left, og_sem, hid_sem,
 ):
     bits, hop_bits, k_bit, per_dev, docs, og_chunk, hid_chunk = plan
     tokens = hid.shape[0]
@@ -35,8 +35,8 @@
             for j, (src, dst) in enumerate(pairs)
         ]
 
-    for pairs, sems, chunk in ((og_pairs, og_sem, og_chunk), (hid_pairs, hid_sem, hid_chunk)):
-        for i in range(pairs[0][0].shape[1] // chunk):
+    for i in range(hid.shape[1] // hid_chunk):
+        for pairs, sems, chunk in ((og_pairs, og_sem, og_chunk), (hid_pairs, hid_sem, hid_chunk)):
             for copy in fetches(i, pairs, sems, chunk)[1]:
                 copy.start()
 
@@ -57,21 +57,22 @@
     inside = (token >= starts) & (token < ends)
     token_row = jnp.sum(jnp.where(inside, row, 0.0), axis=0, keepdims=True)
 
-    def project(pairs, sems, chunk):
-        (src, values), (_, weights) = pairs
-
-        def step(i, total):
-            cols, copies = fetches(i, pairs, sems, chunk)
+    def step(i, totals):
+        fetched = [
+            (pairs, *fetches(i, pairs, sems, chunk))
+            for pairs, sems, chunk in ((og_pairs, og_sem, og_chunk), (hid_pairs, hid_sem, hid_chunk))
+        ]
+        for _, _, copies in fetched:
             for copy in copies:
                 copy.wait()
-            return total + lax.dot_general(
-                weights[:, cols], values[:, cols], NT, preferred_element_type=F32
-            )
-
-        return lax.fori_loop(0, src.shape[1] // chunk, step, jnp.zeros((rank, tokens), F32))
-
-    grad_low = project(og_pairs, og_sem, og_chunk)
-    input_low = project(hid_pairs, hid_sem, hid_chunk)
+        return tuple(
+            total + lax.dot_general(x[:, cols], w[:, cols], NT, preferred_element_type=F32)
+            for total, (((_, x), (_, w)), cols, _) in zip(totals, fetched)
+        )
+
+    zeros = jnp.zeros((tokens, rank), F32)
+    grad_low, input_low = lax.fori_loop(0, hid.shape[1] // hid_chunk, step, (zeros, zeros))
+    grad_low, input_low = grad_low.T, input_low.T
 
     half = rank // 4
     out_r = lax.broadcasted_iota(jnp.int32, (rank, rank), 0)
@@ -95,30 +96,27 @@
             [jnp.concatenate([x, zero], axis=1), jnp.concatenate([zero, x], axis=1)], axis=0
         )
 
-    right_hi = diagonal(x_hi)
-    right_both = jnp.concatenate([right_hi, diagonal(x_lo)], axis=0)
+    right = jnp.concatenate([diagonal(x_hi), diagonal(x_lo)], axis=0)
+    right = jnp.concatenate([right, right], axis=1)
 
     in_block = 2 * per_dev
     blocks = docs // in_block
+    row = 0
     for block in range(blocks):
-        left_hi, left_lo = [], []
         for h in range(2):
             rows = pl.ds(h * half, half)
             for s in range(in_block):
                 entry = block * in_block + (s + h * per_dev) % in_block
                 hit = (token_row == float(entry)).astype(F32).astype(BF16)
                 hit = jnp.concatenate([hit, hit], axis=1)
-                left_hi.append(pair_hi[rows, :] * hit)
-                left_lo.append(pair_lo[rows, :] * hit)
-        left_hi, left_lo = jnp.concatenate(left_hi, axis=0), jnp.concatenate(left_lo, axis=0)
-        both = lax.dot_general(left_hi, right_both, NT, preferred_element_type=F32)
-        low = lax.dot_general(left_lo, right_hi, NT, preferred_element_type=F32)
-        out = both[:, :LANES] + (both[:, LANES:] + low)
-        size = out.shape[0]
-        if block < blocks // 2:
-            keep[pl.ds(block * size, size), :] = out
-        else:
-            send[pl.ds((block - blocks // 2) * size, size), :] = out
+                left[row:row + half, :2 * tokens] = pair_hi[rows, :] * hit
+                left[row:row + half, 2 * tokens:] = pair_lo[rows, :] * hit
+                row += half
+    size = keep.shape[0]
+    for part, out_ref in enumerate((send, keep)):
+        rows = left[(1 - part) * size:(2 - part) * size, :]
+        both = lax.dot_general(rows, right, NT, preferred_element_type=F32)
+        out_ref[...] = both[:, :LANES] + both[:, LANES:]
 
 
 def near_kernel(per_dev, grads_a, grads_b, q, left, out, total):
@@ -173,12 +171,7 @@
     q_send = lax.dynamic_slice_in_dim(queries, (1 - mine) * depth, depth, axis=1)
     q_bits = (k_bit,)
     q_parts = (q_keep, swap(q_send, k_bit))
-    for b in hop_bits[::-1]:
-        q = jnp.concatenate(q_parts, axis=0)
-        q_parts = (q, swap(q, b))
-        q_bits = (b,) + q_bits
-
-    og_chunk, hid_chunk = 2048, 3584
+    og_chunk, hid_chunk = 1024, 3584
     rows = docs * rank * rank // LANES
     any_spec = pl.BlockSpec(memory_space=pl.ANY)
     vmem = pl.BlockSpec(memory_space=pltpu.VMEM)
@@ -195,6 +188,7 @@
             pltpu.VMEM((rank, d), BF16),
             pltpu.VMEM((rank // 2, 2 * tokens), BF16),
             pltpu.VMEM((rank // 2, 2 * tokens), BF16),
+            pltpu.VMEM((rows, 4 * tokens), BF16),
             pltpu.SemaphoreType.DMA((2, d // og_chunk)),
             pltpu.SemaphoreType.DMA((2, ff // hid_chunk)),
         ],
@@ -207,11 +201,19 @@
         name="low",
     )(hidden, out_grad, in_proj.T, out_proj.T, jnp.stack([doc_lengths, doc_slot]))
 
+    sums = []
     for b in hop_bits:
         got = swap(send, b)
         size = keep.shape[0] // 2
         total = keep + got
+        sums.append(total)
         keep, send = total[:size], total[size:]
+    for i, b in enumerate(hop_bits[::-1]):
+        q = jnp.concatenate(q_parts, axis=0)
+        if i == 1:
+            q, _ = lax.optimization_barrier((q, sums[0]))
+        q_parts = (q, swap(q, b))
+        q_bits = (b,) + q_bits
     got = swap(send, k_bit)
 
     width = n * per_q
@@ -226,7 +228,7 @@
         out_specs=(vmem, vmem),
         scratch_shapes=[pltpu.VMEM(keep.shape, F32)],
         compiler_params=pltpu.CompilerParams(vmem_limit_bytes=32 << 20),
-        cost_estimate=pl.CostEstimate(flops=1 << 34, bytes_accessed=1 << 26, transcendentals=0),
+        cost_estimate=pl.CostEstimate(flops=7000000000, bytes_accessed=1 << 20, transcendentals=0),
         name="near_scores",
     )(keep, got, q_parts[0])
     small = jax.ShapeDtypeStruct((per_dev, width), F32)

time: 38 us -> 34.7 us (0.913)
  starting transfers between devices: 15.4 us -> 11.5 us
  Pallas kernels: 9.18 us -> 6.78 us
  waiting for transfers between devices: 11.8 us -> 13.8 us
  local copies, waits for them, and re-layouts: 0.04 us -> 0.94 us
    ppermute x9, starting transfers between devices: 15.4 us -> 11.5 us  [swap(): return lax.ppermute(x, 'ctx', [(i, i ^ 1 << b) for i in range(n)])]
    pallas_call x1, Pallas kernels: 8.54 us -> 6.14 us  [shards(): pl.pallas_call(functools.partial(low_kernel, (bits, hop_bits, k_bit, per_...]
    ppermute x9, waiting for transfers between devices: 11.8 us -> 13.8 us  [swap(): return lax.ppermute(x, 'ctx', [(i, i ^ 1 << b) for i in range(n)])]
    dynamic_slice x1, local copies, waits for them, and re-layouts: 0.01 us -> 0.88 us  [shards(): q_keep = lax.dynamic_slice_in_dim(queries, mine * depth, depth, axis=1)]
  transfers between devices with their start and end apart: 9 -> 9, of which waited for: 6 -> 5; matrix products, arithmetic and copies ran while one was open for 0% -> 2% of each run, Pallas kernels for 1% -> 19%
where the time goes in v3:
time: 34.7 us; the launch traced here: 34.5 us
  waiting for transfers between devices  13.8 us (40%)
  starting transfers between devices  11.5 us (33%)
  Pallas kernels  6.78 us (20%)
  other arithmetic  1.34 us (4%)
  local copies, waits for them, and re-layouts  0.94 us (3%)
    ppermute x9, waiting for transfers between devices, swap(): return lax.ppermute(x, 'ctx', [(i, i ^ 1 << b) for i in range(n)])  13.8 us
    ppermute x9, starting transfers between devices, swap(): return lax.ppermute(x, 'ctx', [(i, i ^ 1 << b) for i in range(n)])  11.5 us
    pallas_call x1, Pallas kernels, shards(): pl.pallas_call(functools.partial(low_kernel, (bits, hop_bits, k_bit, per_...  6.14 us
    dynamic_slice x1, local copies, waits for them, and re-layouts, shards(): q_keep = lax.dynamic_slice_in_dim(queries, mine * depth, depth, axis=1)  0.88 us
  transfers between devices with their start and end apart: 9, of which 5 were waited for; matrix products, arithmetic and copies ran while one was open for 2% of the time, Pallas kernels for 19%

profile of v3, /device:TPU:0, one launch (start us, length us, event | category | flops | bytes accessed | tf_op | source)
XLA Modules:
  0.0 34.5 jit_solution(11791230899272134801)
XLA Ops:
  0.0 0.9 %constant_dynamic-slice_fusion.1 = (bf16[16,2048]{1,0:T(8,128)(2,1)S(1)}, bf16[16,2048]{1,0:T(8,128)(2,1)S(1)}) fusion(bf16[16,4096]{1,0:T(8,128)(2,1)} %param.13, s32[]{:T(128)S(6)} %select_n.6, s32[]{:T(128)S(6)} %select_n.7), kind=kLoop, calls=%fused_computation.8 | loop fusion | bytes 262152 | tf_op jit(solution)/shard_map/dynamic_slice | solution.py:170
  0.9 4.1 %collective-permute-start.4 = (bf16[16,2048]{1,0:T(8,128)(2,1)S(1)}, bf16[16,2048]{1,0:T(8,128)(2,1)S(1)}, u32[]{:S(2)}, u32[]{:S(2)}) collective-permute-start(bf16[16,2048]{1,0:T(8,128)(2,1)S(1)} %get-tuple-element.20), channel_id=1, source_target_pairs={{0,8},{1,9},{2,10},{3,11},{4,12},{5,13},{6,14},{7,15},{8,0},{9,1},... | collective-permute-start | bytes 196616 | tf_op jit(solution)/shard_map/ppermute | solution.py:166
  5.0 0.7 %pad_add_fusion.documents = s32[2,32]{1,0:T(2,128)S(1)} fusion(s32[1,32]{1,0:T(1,128)} %bitcast.6, s32[1,32]{1,0:T(1,128)} %bitcast.7), kind=kLoop, calls=%fused_computation.6 | loop fusion | flops 64 | bytes 512 | tf_op jit(solution)/shard_map/stack | solution.py:202
  5.7 6.1 %low.1 = (f32[512,128]{1,0:T(8,128)S(1)}, f32[512,128]{1,0:T(8,128)S(1)}) custom-call(bf16[256,14336]{1,0:T(8,128)(2,1)} %hid.1, bf16[256,4096]{1,0:T(8,128)(2,1)} %og.1, bf16[64,14336]{1,0:T(8,128)(2,1)} %bitcast.4, bf16[64,4096]{1,0:T(8,128)(2,1)} %bitcast.5, s32[2,32]{1,0:T(2,128)S(1)} %pad_add_fusion.documents), custom_call_target="tpu_custom_call" | custom-call | flops 603979776 | bytes 11796480 | tf_op jit(solution)/shard_map/low/pallas_call | solution.py:179
  11.8 0.1 collective-permute-start
  11.9 0.0 collective-permute-done.4
  11.9 1.6 %collective-permute-start.5 = (bf16[32,2048]{1,0:T(8,128)(2,1)S(1)}, bf16[32,2048]{1,0:T(8,128)(2,1)S(1)}, u32[]{:S(2)}, u32[]{:S(2)}) collective-permute-start(bf16[32,2048]{1,0:T(8,128)(2,1)S(1)} %pad_maximum_fusion.1), channel_id=1, source_target_pairs={{0,4},{1,5},{2,6},{3,7},{4,0},{5,1},{6,2},{7,3},{8,12},{9,13},{10,... | collective-permute-start | bytes 393224 | tf_op jit(solution)/shard_map/ppermute | solution.py:166
  13.6 0.0 collective-permute-done
  13.6 1.6 %collective-permute-start.1 = (f32[256,128]{1,0:T(8,128)S(1)}, f32[256,128]{1,0:T(8,128)S(1)}, u32[]{:S(2)}, u32[]{:S(2)}) collective-permute-start(f32[256,128]{1,0:T(8,128)S(1)} %slice.25), channel_id=1, source_target_pairs={{0,2},{1,3},{2,0},{3,1},{4,6},{5,7},{6,4},{7,5},{8,10},{9,11},{10,... | collective-permute-start | bytes 393224 | tf_op jit(solution)/shard_map/ppermute | solution.py:166
  15.2 2.7 %collective-permute-done.5 = bf16[32,2048]{1,0:T(8,128)(2,1)S(1)} collective-permute-done((bf16[32,2048]{1,0:T(8,128)(2,1)S(1)}, bf16[32,2048]{1,0:T(8,128)(2,1)S(1)}, u32[]{:S(2)}, u32[]{:S(2)}) %collective-permute-start.5) | collective-permute-done | bytes 131104 | tf_op jit(solution)/shard_map/ppermute | solution.py:166
  17.9 1.6 %collective-permute-start.6 = (bf16[64,2048]{1,0:T(8,128)(2,1)S(1)}, bf16[64,2048]{1,0:T(8,128)(2,1)S(1)}, u32[]{:S(2)}, u32[]{:S(2)}) collective-permute-start(bf16[64,2048]{1,0:T(8,128)(2,1)S(1)} %pad_maximum_fusion), channel_id=1, source_target_pairs={{0,2},{1,3},{2,0},{3,1},{4,6},{5,7},{6,4},{7,5},{8,10},{9,11},{10,... | collective-permute-start | bytes 786440 | tf_op jit(solution)/shard_map/ppermute | solution.py:166
  19.5 0.0 collective-permute-done.1
  19.5 1.6 %collective-permute-start.2 = (f32[128,128]{1,0:T(8,128)S(1)}, f32[128,128]{1,0:T(8,128)S(1)}, u32[]{:S(2)}, u32[]{:S(2)}) collective-permute-start(f32[128,128]{1,0:T(8,128)S(1)} %slice.27), channel_id=1, source_target_pairs={{0,4},{1,5},{2,6},{3,7},{4,0},{5,1},{6,2},{7,3},{8,12},{9,13},{10,... | collective-permute-start | bytes 196616 | tf_op jit(solution)/shard_map/ppermute | solution.py:166
  21.2 2.7 %collective-permute-done.2 = f32[128,128]{1,0:T(8,128)S(1)} collective-permute-done((f32[128,128]{1,0:T(8,128)S(1)}, f32[128,128]{1,0:T(8,128)S(1)}, u32[]{:S(2)}, u32[]{:S(2)}) %collective-permute-start.2) | collective-permute-done | bytes 65568 | tf_op jit(solution)/shard_map/ppermute | solution.py:166
  23.9 0.4 %collective-permute-start.3 = (f32[64,128]{1,0:T(8,128)S(1)}, f32[64,128]{1,0:T(8,128)S(1)}, u32[]{:S(2)}, u32[]{:S(2)}) collective-permute-start(f32[64,128]{1,0:T(8,128)S(1)} %get-tuple-element.21), channel_id=1, source_target_pairs={{0,8},{1,9},{2,10},{3,11},{4,12},{5,13},{6,14},{7,15},{8,0},{9,1},... | collective-permute-start | bytes 98312 | tf_op jit(solution)/shard_map/ppermute | solution.py:166
  24.3 1.6 %collective-permute-done.6 = bf16[64,2048]{1,0:T(8,128)(2,1)S(1)} collective-permute-done((bf16[64,2048]{1,0:T(8,128)(2,1)S(1)}, bf16[64,2048]{1,0:T(8,128)(2,1)S(1)}, u32[]{:S(2)}, u32[]{:S(2)}) %collective-permute-start.6) | collective-permute-done | bytes 262176 | tf_op jit(solution)/shard_map/ppermute | solution.py:166
  25.9 0.1 collective-permute-start.7
  26.0 2.8 %collective-permute-done.3.grads_b = f32[64,128]{1,0:T(8,128)S(1)} collective-permute-done((f32[64,128]{1,0:T(8,128)S(1)}, f32[64,128]{1,0:T(8,128)S(1)}, u32[]{:S(2)}, u32[]{:S(2)}) %collective-permute-start.3) | collective-permute-done | bytes 32800 | tf_op jit(solution)/shard_map/ppermute | solution.py:166
  28.8 0.3 near_scores.1
  29.1 0.0 collective-permute-done.7.q_b
  29.1 0.3 scores.1
  29.4 0.4 %collective-permute-start.8 = (f32[2,256]{1,0:T(2,128)S(1)}, f32[2,256]{1,0:T(2,128)S(1)}, u32[]{:S(2)}, u32[]{:S(2)}) collective-permute-start(f32[2,256]{1,0:T(2,128)S(1)} %get-tuple-element.18), channel_id=1, source_target_pairs={{0,8},{1,9},{2,10},{3,11},{4,12},{5,13},{6,14},{7,15},{8,0},{9,1},... | collective-permute-start | bytes 6152 | tf_op jit(solution)/shard_map/ppermute | solution.py:166
  29.8 4.1 %collective-permute-done.8 = f32[2,256]{1,0:T(2,128)S(1)} collective-permute-done((f32[2,256]{1,0:T(2,128)S(1)}, f32[2,256]{1,0:T(2,128)S(1)}, u32[]{:S(2)}, u32[]{:S(2)}) %collective-permute-start.8) | collective-permute-done | bytes 2080 | tf_op jit(solution)/shard_map/ppermute | solution.py:166
  33.9 0.6 %add.23 = f32[2,256]{1,0:T(2,128)} add(f32[2,256]{1,0:T(2,128)S(1)} %get-tuple-element.17, f32[2,256]{1,0:T(2,128)S(1)} %collective-permute-done.8) | non-fusion elementwise | flops 512 | bytes 6144 | tf_op jit(solution)/shard_map/add | solution.py:244
  (10 shorter events, 0.1 us)
Async XLA Ops:
  0.9 11.0 %collective-permute-start.4 = (bf16[16,2048]{1,0:T(8,128)(2,1)S(1)}, bf16[16,2048]{1,0:T(8,128)(2,1)S(1)}, u32[]{:S(2)}, u32[]{:S(2)}) collective-permute-start(bf16[16,2048]{1,0:T(8,128)(2,1)S(1)} %get-tuple-element.20), channel_id=1, source_target_pairs={{0,8},{1,9},{2,10},{3,11},{4,12},{5,13},{6,14},{7,15},{8,0},{9,1},... | collective-permute-start | bytes 196616 | tf_op jit(solution)/shard_map/ppermute | solution.py:166
  11.8 1.8 %collective-permute-start = (f32[512,128]{1,0:T(8,128)S(1)}, f32[512,128]{1,0:T(8,128)S(1)}, u32[]{:S(2)}, u32[]{:S(2)}) collective-permute-start(f32[512,128]{1,0:T(8,128)S(1)} %get-tuple-element.13), channel_id=1, source_target_pairs={{0,1},{1,0},{2,3},{3,2},{4,5},{5,4},{6,7},{7,6},{8,9},{9,8},{10,11... | collective-permute-start | bytes 786440 | tf_op jit(solution)/shard_map/ppermute | solution.py:166
  11.9 6.0 %collective-permute-start.5 = (bf16[32,2048]{1,0:T(8,128)(2,1)S(1)}, bf16[32,2048]{1,0:T(8,128)(2,1)S(1)}, u32[]{:S(2)}, u32[]{:S(2)}) collective-permute-start(bf16[32,2048]{1,0:T(8,128)(2,1)S(1)} %pad_maximum_fusion.1), channel_id=1, source_target_pairs={{0,4},{1,5},{2,6},{3,7},{4,0},{5,1},{6,2},{7,3},{8,12},{9,13},{10,... | collective-permute-start | bytes 393224 | tf_op jit(solution)/shard_map/ppermute | solution.py:166
  13.6 5.9 %collective-permute-start.1 = (f32[256,128]{1,0:T(8,128)S(1)}, f32[256,128]{1,0:T(8,128)S(1)}, u32[]{:S(2)}, u32[]{:S(2)}) collective-permute-start(f32[256,128]{1,0:T(8,128)S(1)} %slice.25), channel_id=1, source_target_pairs={{0,2},{1,3},{2,0},{3,1},{4,6},{5,7},{6,4},{7,5},{8,10},{9,11},{10,... | collective-permute-start | bytes 393224 | tf_op jit(solution)/shard_map/ppermute | solution.py:166
  17.9 8.0 %collective-permute-start.6 = (bf16[64,2048]{1,0:T(8,128)(2,1)S(1)}, bf16[64,2048]{1,0:T(8,128)(2,1)S(1)}, u32[]{:S(2)}, u32[]{:S(2)}) collective-permute-start(bf16[64,2048]{1,0:T(8,128)(2,1)S(1)} %pad_maximum_fusion), channel_id=1, source_target_pairs={{0,2},{1,3},{2,0},{3,1},{4,6},{5,7},{6,4},{7,5},{8,10},{9,11},{10,... | collective-permute-start | bytes 786440 | tf_op jit(solution)/shard_map/ppermute | solution.py:166
  19.5 4.3 %collective-permute-start.2 = (f32[128,128]{1,0:T(8,128)S(1)}, f32[128,128]{1,0:T(8,128)S(1)}, u32[]{:S(2)}, u32[]{:S(2)}) collective-permute-start(f32[128,128]{1,0:T(8,128)S(1)} %slice.27), channel_id=1, source_target_pairs={{0,4},{1,5},{2,6},{3,7},{4,0},{5,1},{6,2},{7,3},{8,12},{9,13},{10,... | collective-permute-start | bytes 196616 | tf_op jit(solution)/shard_map/ppermute | solution.py:166
  23.9 4.9 %collective-permute-start.3 = (f32[64,128]{1,0:T(8,128)S(1)}, f32[64,128]{1,0:T(8,128)S(1)}, u32[]{:S(2)}, u32[]{:S(2)}) collective-permute-start(f32[64,128]{1,0:T(8,128)S(1)} %get-tuple-element.21), channel_id=1, source_target_pairs={{0,8},{1,9},{2,10},{3,11},{4,12},{5,13},{6,14},{7,15},{8,0},{9,1},... | collective-permute-start | bytes 98312 | tf_op jit(solution)/shard_map/ppermute | solution.py:166
  25.9 3.2 %collective-permute-start.7 = (bf16[128,2048]{1,0:T(8,128)(2,1)S(1)}, bf16[128,2048]{1,0:T(8,128)(2,1)S(1)}, u32[]{:S(2)}, u32[]{:S(2)}) collective-permute-start(bf16[128,2048]{1,0:T(8,128)(2,1)S(1)} %constant_dynamic-update-slice_fusion.q), channel_id=1, source_target_pairs={{0,1},{1,0},{2,3},{3,2},{4,5},{5,4},{6,7},{7,6},{8,9},{9,8},{10,11... | collective-permute-start | bytes 1572872 | tf_op jit(solution)/shard_map/ppermute | solution.py:166
  29.4 4.5 %collective-permute-start.8 = (f32[2,256]{1,0:T(2,128)S(1)}, f32[2,256]{1,0:T(2,128)S(1)}, u32[]{:S(2)}, u32[]{:S(2)}) collective-permute-start(f32[2,256]{1,0:T(2,128)S(1)} %get-tuple-element.18), channel_id=1, source_target_pairs={{0,8},{1,9},{2,10},{3,11},{4,12},{5,13},{6,14},{7,15},{8,0},{9,1},... | collective-permute-start | bytes 6152 | tf_op jit(solution)/shard_map/ppermute | solution.py:166

commit v4 on v3

--- a/solution.py
+++ b/solution.py
@@ -65,13 +65,21 @@
         for _, _, copies in fetched:
             for copy in copies:
                 copy.wait()
+        (_, og_cols, _), (_, hid_cols, _) = fetched
+        start, size = hid_cols.start, hid_chunk // 2
+        parts = (
+            (og_v, w_out_v, og_cols),
+            (hid_v, w_in_v, pl.ds(start, size)),
+            (hid_v, w_in_v, pl.ds(pl.multiple_of(start + size, size), size)),
+        )
         return tuple(
             total + lax.dot_general(x[:, cols], w[:, cols], NT, preferred_element_type=F32)
-            for total, (((_, x), (_, w)), cols, _) in zip(totals, fetched)
+            for total, (x, w, cols) in zip(totals, parts)
         )
 
     zeros = jnp.zeros((tokens, rank), F32)
-    grad_low, input_low = lax.fori_loop(0, hid.shape[1] // hid_chunk, step, (zeros, zeros))
+    grad_low, first, second = lax.fori_loop(0, hid.shape[1] // hid_chunk, step, (zeros,) * 3)
+    input_low = first + second
     grad_low, input_low = grad_low.T, input_low.T
 
     half = rank // 4
@@ -158,8 +166,8 @@
     docs = doc_slot.shape[0]
     per_dev = docs // n
     per_q = queries.shape[0]
-    k_bit = bits - 1
-    hop_bits = tuple(range(bits - 1))
+    k_bit, top = 2, bits - 1
+    hop_bits = tuple(b for b in range(bits) if b != k_bit)
     me = lax.axis_index("ctx")
 
     def swap(x, b):
@@ -167,10 +175,7 @@
 
     depth = queries.shape[1] // 2
     mine = (me >> k_bit) & 1
-    q_keep = lax.dynamic_slice_in_dim(queries, mine * depth, depth, axis=1)
-    q_send = lax.dynamic_slice_in_dim(queries, (1 - mine) * depth, depth, axis=1)
-    q_bits = (k_bit,)
-    q_parts = (q_keep, swap(q_send, k_bit))
+    got_queries = swap(queries, top)
     og_chunk, hid_chunk = 1024, 3584
     rows = docs * rank * rank // LANES
     any_spec = pl.BlockSpec(memory_space=pl.ANY)
@@ -208,9 +213,15 @@
         total = keep + got
         sums.append(total)
         keep, send = total[:size], total[size:]
-    for i, b in enumerate(hop_bits[::-1]):
+    q = jnp.concatenate([queries, got_queries], axis=0)
+    q_keep = lax.dynamic_slice_in_dim(q, mine * depth, depth, axis=1)
+    q_send = lax.dynamic_slice_in_dim(q, (1 - mine) * depth, depth, axis=1)
+    q_bits = (k_bit, top)
+    q_parts = (q_keep, swap(q_send, k_bit))
+    rest = tuple(b for b in hop_bits[::-1] if b != top)
+    for i, b in enumerate(rest):
         q = jnp.concatenate(q_parts, axis=0)
-        if i == 1:
+        if i == 0:
             q, _ = lax.optimization_barrier((q, sums[0]))
         q_parts = (q, swap(q, b))
         q_bits = (b,) + q_bits

time: 34.7 us -> 33.1 us (0.954)
  waiting for transfers between devices: 13.8 us -> 11.2 us
  starting transfers between devices: 11.5 us -> 13.4 us
  local copies, waits for them, and re-layouts: 0.94 us -> 0.11 us
    ppermute x9, waiting for transfers between devices: 13.8 us -> 11.2 us  [swap(): return lax.ppermute(x, 'ctx', [(i, i ^ 1 << b) for i in range(n)])]
    ppermute x9, starting transfers between devices: 11.5 us -> 13.4 us  [swap(): return lax.ppermute(x, 'ctx', [(i, i ^ 1 << b) for i in range(n)])]
    dynamic_slice x1, local copies, waits for them, and re-layouts: 0.88 us -> 0.03 us  [shards(): q_keep = lax.dynamic_slice_in_dim(q, mine * depth, depth, axis=1)]
  transfers between devices with their start and end apart: 9 -> 9, of which waited for: 5 -> 4; matrix products, arithmetic and copies ran while one was open for 2% -> 3% of each run, Pallas kernels for 19% -> 20%
where the time goes in v4:
time: 33.1 us; the launch traced here: 33 us
  starting transfers between devices  13.4 us (40%)
  waiting for transfers between devices  11.2 us (34%)
  Pallas kernels  6.82 us (21%)
  other arithmetic  1.33 us (4%)
    ppermute x9, starting transfers between devices, swap(): return lax.ppermute(x, 'ctx', [(i, i ^ 1 << b) for i in range(n)])  13.4 us
    ppermute x9, waiting for transfers between devices, swap(): return lax.ppermute(x, 'ctx', [(i, i ^ 1 << b) for i in range(n)])  11.2 us
    pallas_call x1, Pallas kernels, shards(): pl.pallas_call(functools.partial(low_kernel, (bits, hop_bits, k_bit, per_...  6.17 us
    another operation x1, other arithmetic, shards(): jnp.stack([doc_lengths, doc_slot])  0.68 us
  transfers between devices with their start and end apart: 9, of which 4 were waited for; matrix products, arithmetic and copies ran while one was open for 3% of the time, Pallas kernels for 20%

profile of v4, /device:TPU:0, one launch (start us, length us, event | category | flops | bytes accessed | tf_op | source)
XLA Modules:
  0.0 33.0 jit_solution(18234851340394568316)
XLA Ops:
  0.0 4.0 %collective-permute-start.4 = (bf16[16,4096]{1,0:T(8,128)(2,1)}, bf16[16,4096]{1,0:T(8,128)(2,1)S(1)}, u32[]{:S(2)}, u32[]{:S(2)}) collective-permute-start(bf16[16,4096]{1,0:T(8,128)(2,1)} %param.13), channel_id=1, source_target_pairs={{0,8},{1,9},{2,10},{3,11},{4,12},{5,13},{6,14},{7,15},{8,0},{9,1},... | collective-permute-start | bytes 393224 | tf_op jit(solution)/shard_map/ppermute | solution.py:174
  4.0 0.7 %pad_add_fusion.documents = s32[2,32]{1,0:T(2,128)S(1)} fusion(s32[1,32]{1,0:T(1,128)} %bitcast.6, s32[1,32]{1,0:T(1,128)} %bitcast.7), kind=kLoop, calls=%fused_computation.7 | loop fusion | flops 64 | bytes 512 | tf_op jit(solution)/shard_map/stack | solution.py:207
  4.7 0.0 copy-start
  4.7 6.2 %low.1 = (f32[512,128]{1,0:T(8,128)S(1)}, f32[512,128]{1,0:T(8,128)S(1)}) custom-call(bf16[256,14336]{1,0:T(8,128)(2,1)} %hid.1, bf16[256,4096]{1,0:T(8,128)(2,1)} %og.1, bf16[64,14336]{1,0:T(8,128)(2,1)} %bitcast.4, bf16[64,4096]{1,0:T(8,128)(2,1)} %bitcast.5, s32[2,32]{1,0:T(2,128)S(1)} %pad_add_fusion.documents), custom_call_target="tpu_custom_call" | custom-call | flops 603979776 | bytes 11796480 | tf_op jit(solution)/shard_map/low/pallas_call | solution.py:184
  10.9 0.1 collective-permute-start
  11.0 0.0 copy-done
  11.0 0.0 collective-permute-done.4
  11.1 1.6 %collective-permute-start.5 = (bf16[32,2048]{1,0:T(8,128)(2,1)S(1)}, bf16[32,2048]{1,0:T(8,128)(2,1)S(1)}, u32[]{:S(2)}, u32[]{:S(2)}) collective-permute-start(bf16[32,2048]{1,0:T(8,128)(2,1)S(1)} %get-tuple-element.20), channel_id=1, source_target_pairs={{0,4},{1,5},{2,6},{3,7},{4,0},{5,1},{6,2},{7,3},{8,12},{9,13},{10,... | collective-permute-start | bytes 393224 | tf_op jit(solution)/shard_map/ppermute | solution.py:174
  12.7 0.0 collective-permute-done
  12.8 1.6 %collective-permute-start.1 = (f32[256,128]{1,0:T(8,128)S(1)}, f32[256,128]{1,0:T(8,128)S(1)}, u32[]{:S(2)}, u32[]{:S(2)}) collective-permute-start(f32[256,128]{1,0:T(8,128)S(1)} %slice.25), channel_id=1, source_target_pairs={{0,2},{1,3},{2,0},{3,1},{4,6},{5,7},{6,4},{7,5},{8,10},{9,11},{10,... | collective-permute-start | bytes 393224 | tf_op jit(solution)/shard_map/ppermute | solution.py:174
  14.4 2.7 %collective-permute-done.5 = bf16[32,2048]{1,0:T(8,128)(2,1)S(1)} collective-permute-done((bf16[32,2048]{1,0:T(8,128)(2,1)S(1)}, bf16[32,2048]{1,0:T(8,128)(2,1)S(1)}, u32[]{:S(2)}, u32[]{:S(2)}) %collective-permute-start.5) | collective-permute-done | bytes 131104 | tf_op jit(solution)/shard_map/ppermute | solution.py:174
  17.1 1.6 %collective-permute-start.6 = (bf16[64,2048]{1,0:T(8,128)(2,1)S(1)}, bf16[64,2048]{1,0:T(8,128)(2,1)S(1)}, u32[]{:S(2)}, u32[]{:S(2)}) collective-permute-start(bf16[64,2048]{1,0:T(8,128)(2,1)S(1)} %pad_maximum_fusion), channel_id=1, source_target_pairs={{0,2},{1,3},{2,0},{3,1},{4,6},{5,7},{6,4},{7,5},{8,10},{9,11},{10,... | collective-permute-start | bytes 786440 | tf_op jit(solution)/shard_map/ppermute | solution.py:174
  18.6 0.0 collective-permute-done.1
  18.7 1.5 %collective-permute-start.2 = (f32[128,128]{1,0:T(8,128)S(1)}, f32[128,128]{1,0:T(8,128)S(1)}, u32[]{:S(2)}, u32[]{:S(2)}) collective-permute-start(f32[128,128]{1,0:T(8,128)S(1)} %slice.27), channel_id=1, source_target_pairs={{0,8},{1,9},{2,10},{3,11},{4,12},{5,13},{6,14},{7,15},{8,0},{9,1},... | collective-permute-start | bytes 196616 | tf_op jit(solution)/shard_map/ppermute | solution.py:174
  20.2 3.9 %collective-permute-done.2 = f32[128,128]{1,0:T(8,128)S(1)} collective-permute-done((f32[128,128]{1,0:T(8,128)S(1)}, f32[128,128]{1,0:T(8,128)S(1)}, u32[]{:S(2)}, u32[]{:S(2)}) %collective-permute-start.2) | collective-permute-done | bytes 65568 | tf_op jit(solution)/shard_map/ppermute | solution.py:174
  24.1 1.5 %collective-permute-start.3 = (f32[64,128]{1,0:T(8,128)S(1)}, f32[64,128]{1,0:T(8,128)S(1)}, u32[]{:S(2)}, u32[]{:S(2)}) collective-permute-start(f32[64,128]{1,0:T(8,128)S(1)} %get-tuple-element.21), channel_id=1, source_target_pairs={{0,4},{1,5},{2,6},{3,7},{4,0},{5,1},{6,2},{7,3},{8,12},{9,13},{10,... | collective-permute-start | bytes 98312 | tf_op jit(solution)/shard_map/ppermute | solution.py:174
  25.6 0.0 collective-permute-done.6
  25.6 0.1 collective-permute-start.7
  25.7 2.4 %collective-permute-done.3.grads_b = f32[64,128]{1,0:T(8,128)S(1)} collective-permute-done((f32[64,128]{1,0:T(8,128)S(1)}, f32[64,128]{1,0:T(8,128)S(1)}, u32[]{:S(2)}, u32[]{:S(2)}) %collective-permute-start.3) | collective-permute-done | bytes 32800 | tf_op jit(solution)/shard_map/ppermute | solution.py:174
  28.1 0.3 near_scores.1
  28.4 0.0 collective-permute-done.7.q_b
  28.4 0.3 %scores.1 = (f32[2,256]{1,0:T(2,128)S(1)}, f32[2,256]{1,0:T(2,128)S(1)}) custom-call(bf16[16,2048]{1,0:T(8,128)(2,1)S(1)} %get-tuple-element.15.left, f32[128,16]{1,0:T(8,128)S(1)} %get-tuple-element.16.out_a, bf16[128,2048]{1,0:T(8,128)(2,1)S(1)} %collective-permute-done.7.q_b), custom_call_target="tpu_custom_call" | custom-call | tf_op jit(solution)/shard_map/scores/pallas_call | solution.py:246
  28.7 1.5 %collective-permute-start.8 = (f32[2,256]{1,0:T(2,128)S(1)}, f32[2,256]{1,0:T(2,128)S(1)}, u32[]{:S(2)}, u32[]{:S(2)}) collective-permute-start(f32[2,256]{1,0:T(2,128)S(1)} %get-tuple-element.18), channel_id=1, source_target_pairs={{0,4},{1,5},{2,6},{3,7},{4,0},{5,1},{6,2},{7,3},{8,12},{9,13},{10,... | collective-permute-start | bytes 6152 | tf_op jit(solution)/shard_map/ppermute | solution.py:174
  30.2 2.2 %collective-permute-done.8 = f32[2,256]{1,0:T(2,128)S(1)} collective-permute-done((f32[2,256]{1,0:T(2,128)S(1)}, f32[2,256]{1,0:T(2,128)S(1)}, u32[]{:S(2)}, u32[]{:S(2)}) %collective-permute-start.8) | collective-permute-done | bytes 2080 | tf_op jit(solution)/shard_map/ppermute | solution.py:174
  32.4 0.6 %add.23 = f32[2,256]{1,0:T(2,128)} add(f32[2,256]{1,0:T(2,128)S(1)} %get-tuple-element.17, f32[2,256]{1,0:T(2,128)S(1)} %collective-permute-done.8) | non-fusion elementwise | flops 512 | bytes 6144 | tf_op jit(solution)/shard_map/add | solution.py:255
  (12 shorter events, 0.2 us)
Async XLA Ops:
  0.0 11.0 %collective-permute-start.4 = (bf16[16,4096]{1,0:T(8,128)(2,1)}, bf16[16,4096]{1,0:T(8,128)(2,1)S(1)}, u32[]{:S(2)}, u32[]{:S(2)}) collective-permute-start(bf16[16,4096]{1,0:T(8,128)(2,1)} %param.13), channel_id=1, source_target_pairs={{0,8},{1,9},{2,10},{3,11},{4,12},{5,13},{6,14},{7,15},{8,0},{9,1},... | collective-permute-start | bytes 393224 | tf_op jit(solution)/shard_map/ppermute | solution.py:174
  4.7 6.3 %copy-start = (bf16[16,4096]{1,0:T(8,128)(2,1)S(1)}, bf16[16,4096]{1,0:T(8,128)(2,1)}, u32[]{:S(2)}) copy-start(bf16[16,4096]{1,0:T(8,128)(2,1)} %param.13) | copy-start | bytes 393220
  10.9 1.8 %collective-permute-start = (f32[512,128]{1,0:T(8,128)S(1)}, f32[512,128]{1,0:T(8,128)S(1)}, u32[]{:S(2)}, u32[]{:S(2)}) collective-permute-start(f32[512,128]{1,0:T(8,128)S(1)} %get-tuple-element.13), channel_id=1, source_target_pairs={{0,1},{1,0},{2,3},{3,2},{4,5},{5,4},{6,7},{7,6},{8,9},{9,8},{10,11... | collective-permute-start | bytes 786440 | tf_op jit(solution)/shard_map/ppermute | solution.py:174
  11.1 6.0 %collective-permute-start.5 = (bf16[32,2048]{1,0:T(8,128)(2,1)S(1)}, bf16[32,2048]{1,0:T(8,128)(2,1)S(1)}, u32[]{:S(2)}, u32[]{:S(2)}) collective-permute-start(bf16[32,2048]{1,0:T(8,128)(2,1)S(1)} %get-tuple-element.20), channel_id=1, source_target_pairs={{0,4},{1,5},{2,6},{3,7},{4,0},{5,1},{6,2},{7,3},{8,12},{9,13},{10,... | collective-permute-start | bytes 393224 | tf_op jit(solution)/shard_map/ppermute | solution.py:174
  12.8 5.9 %collective-permute-start.1 = (f32[256,128]{1,0:T(8,128)S(1)}, f32[256,128]{1,0:T(8,128)S(1)}, u32[]{:S(2)}, u32[]{:S(2)}) collective-permute-start(f32[256,128]{1,0:T(8,128)S(1)} %slice.25), channel_id=1, source_target_pairs={{0,2},{1,3},{2,0},{3,1},{4,6},{5,7},{6,4},{7,5},{8,10},{9,11},{10,... | collective-permute-start | bytes 393224 | tf_op jit(solution)/shard_map/ppermute | solution.py:174
  17.1 8.5 %collective-permute-start.6 = (bf16[64,2048]{1,0:T(8,128)(2,1)S(1)}, bf16[64,2048]{1,0:T(8,128)(2,1)S(1)}, u32[]{:S(2)}, u32[]{:S(2)}) collective-permute-start(bf16[64,2048]{1,0:T(8,128)(2,1)S(1)} %pad_maximum_fusion), channel_id=1, source_target_pairs={{0,2},{1,3},{2,0},{3,1},{4,6},{5,7},{6,4},{7,5},{8,10},{9,11},{10,... | collective-permute-start | bytes 786440 | tf_op jit(solution)/shard_map/ppermute | solution.py:174
  18.7 5.4 %collective-permute-start.2 = (f32[128,128]{1,0:T(8,128)S(1)}, f32[128,128]{1,0:T(8,128)S(1)}, u32[]{:S(2)}, u32[]{:S(2)}) collective-permute-start(f32[128,128]{1,0:T(8,128)S(1)} %slice.27), channel_id=1, source_target_pairs={{0,8},{1,9},{2,10},{3,11},{4,12},{5,13},{6,14},{7,15},{8,0},{9,1},... | collective-permute-start | bytes 196616 | tf_op jit(solution)/shard_map/ppermute | solution.py:174
  24.1 4.0 %collective-permute-start.3 = (f32[64,128]{1,0:T(8,128)S(1)}, f32[64,128]{1,0:T(8,128)S(1)}, u32[]{:S(2)}, u32[]{:S(2)}) collective-permute-start(f32[64,128]{1,0:T(8,128)S(1)} %get-tuple-element.21), channel_id=1, source_target_pairs={{0,4},{1,5},{2,6},{3,7},{4,0},{5,1},{6,2},{7,3},{8,12},{9,13},{10,... | collective-permute-start | bytes 98312 | tf_op jit(solution)/shard_map/ppermute | solution.py:174
  25.6 2.8 %collective-permute-start.7 = (bf16[128,2048]{1,0:T(8,128)(2,1)S(1)}, bf16[128,2048]{1,0:T(8,128)(2,1)S(1)}, u32[]{:S(2)}, u32[]{:S(2)}) collective-permute-start(bf16[128,2048]{1,0:T(8,128)(2,1)S(1)} %constant_dynamic-update-slice_fusion.2.q), channel_id=1, source_target_pairs={{0,1},{1,0},{2,3},{3,2},{4,5},{5,4},{6,7},{7,6},{8,9},{9,8},{10,11... | collective-permute-start | bytes 1572872 | tf_op jit(solution)/shard_map/ppermute | solution.py:174
  28.7 3.6 %collective-permute-start.8 = (f32[2,256]{1,0:T(2,128)S(1)}, f32[2,256]{1,0:T(2,128)S(1)}, u32[]{:S(2)}, u32[]{:S(2)}) collective-permute-start(f32[2,256]{1,0:T(2,128)S(1)} %get-tuple-element.18), channel_id=1, source_target_pairs={{0,4},{1,5},{2,6},{3,7},{4,0},{5,1},{6,2},{7,3},{8,12},{9,13},{10,... | collective-permute-start | bytes 6152 | tf_op jit(solution)/shard_map/ppermute | solution.py:174

commit v5 on v4

--- a/solution.py
+++ b/solution.py
@@ -18,14 +18,11 @@
 
 
 def low_kernel(
-    plan, hid, og, w_in, w_out, documents, keep, send,
-    hid_v, og_v, w_in_v, w_out_v, pair_hi, pair_lo, left, og_sem, hid_sem,
+    og_chunk, hid_chunk, hid, og, w_in, w_out, grad_low, input_low,
+    hid_v, og_v, w_in_v, w_out_v, og_sem, hid_sem,
 ):
-    bits, hop_bits, k_bit, per_dev, docs, og_chunk, hid_chunk = plan
     tokens = hid.shape[0]
     rank = w_in.shape[0]
-    me = lax.axis_index("ctx")
-
     og_pairs, hid_pairs = ((og, og_v), (w_out, w_out_v)), ((hid, hid_v), (w_in, w_in_v))
 
     def fetches(i, pairs, sems, chunk):
@@ -39,23 +36,6 @@
         for pairs, sems, chunk in ((og_pairs, og_sem, og_chunk), (hid_pairs, hid_sem, hid_chunk)):
             for copy in fetches(i, pairs, sems, chunk)[1]:
                 copy.start()
-
-    lane = lax.broadcasted_iota(jnp.int32, (docs, docs), 1)
-    sub = lax.broadcasted_iota(jnp.int32, (docs, docs), 0)
-    length = jnp.broadcast_to(documents[0:1, :], (docs, docs)).astype(F32)
-    slot = jnp.broadcast_to(documents[1:2, :], (docs, docs)).astype(F32)
-    ends = jnp.sum(jnp.where(lane <= sub, length, 0.0), axis=1, keepdims=True)
-    starts = jnp.sum(jnp.where(lane < sub, length, 0.0), axis=1, keepdims=True)
-    slot = jnp.sum(jnp.where(lane == sub, slot, 0.0), axis=1, keepdims=True).astype(jnp.int32)
-    owner = slot // per_dev
-    apart = owner ^ me
-    row = jnp.zeros_like(slot)
-    for b in hop_bits + (k_bit,):
-        row = row * 2 + ((apart >> b) & 1)
-    row = (row * per_dev + (slot - owner * per_dev)).astype(F32)
-    token = (me * tokens + lax.broadcasted_iota(jnp.int32, (docs, tokens), 1)).astype(F32)
-    inside = (token >= starts) & (token < ends)
-    token_row = jnp.sum(jnp.where(inside, row, 0.0), axis=0, keepdims=True)
 
     def step(i, totals):
         fetched = [
@@ -78,9 +58,33 @@
         )
 
     zeros = jnp.zeros((tokens, rank), F32)
-    grad_low, first, second = lax.fori_loop(0, hid.shape[1] // hid_chunk, step, (zeros,) * 3)
-    input_low = first + second
-    grad_low, input_low = grad_low.T, input_low.T
+    grad, first, second = lax.fori_loop(0, hid.shape[1] // hid_chunk, step, (zeros,) * 3)
+    grad_low[...], input_low[...] = grad.T, (first + second).T
+
+
+def outer_kernel(
+    plan, grad_low, input_low, lengths, slots, keep, send, pair_hi, pair_lo, left
+):
+    hop_bits, k_bit, per_dev, docs = plan
+    rank, tokens = grad_low.shape
+    me = lax.axis_index("ctx")
+
+    lane = lax.broadcasted_iota(jnp.int32, (docs, docs), 1)
+    sub = lax.broadcasted_iota(jnp.int32, (docs, docs), 0)
+    length = jnp.broadcast_to(lengths[...], (docs, docs)).astype(F32)
+    slot = jnp.broadcast_to(slots[...], (docs, docs)).astype(F32)
+    ends = jnp.sum(jnp.where(lane <= sub, length, 0.0), axis=1, keepdims=True)
+    starts = jnp.sum(jnp.where(lane < sub, length, 0.0), axis=1, keepdims=True)
+    slot = jnp.sum(jnp.where(lane == sub, slot, 0.0), axis=1, keepdims=True).astype(jnp.int32)
+    owner = slot // per_dev
+    apart = owner ^ me
+    row = jnp.zeros_like(slot)
+    for b in hop_bits + (k_bit,):
+        row = row * 2 + ((apart >> b) & 1)
+    row = (row * per_dev + (slot - owner * per_dev)).astype(F32)
+    token = (me * tokens + lax.broadcasted_iota(jnp.int32, (docs, tokens), 1)).astype(F32)
+    inside = (token >= starts) & (token < ends)
+    token_row = jnp.sum(jnp.where(inside, row, 0.0), axis=0, keepdims=True)
 
     half = rank // 4
     out_r = lax.broadcasted_iota(jnp.int32, (rank, rank), 0)
@@ -89,14 +93,14 @@
     mine = (me >> k_bit) & 1
     p = (p // half ^ mine) * half + p % half
     order = (in_r == 2 * p + odd).astype(BF16)
-    g_hi, g_lo = split2(grad_low)
+    g_hi, g_lo = split2(grad_low[...])
     g_hi = jnp.dot(order, g_hi, preferred_element_type=F32).astype(BF16)
     g_lo = jnp.dot(order, g_lo, preferred_element_type=F32).astype(BF16)
     pairs = rank // 2
     pair_hi[:, :tokens], pair_hi[:, tokens:] = g_hi[:pairs], g_hi[pairs:]
     pair_lo[:, :tokens], pair_lo[:, tokens:] = g_lo[:pairs], g_lo[pairs:]
 
-    x_hi, x_lo = split2(input_low)
+    x_hi, x_lo = split2(input_low[...])
     zero = jnp.zeros_like(x_hi)
 
     def diagonal(x):
@@ -107,14 +111,14 @@
     right = jnp.concatenate([diagonal(x_hi), diagonal(x_lo)], axis=0)
     right = jnp.concatenate([right, right], axis=1)
 
-    in_block = 2 * per_dev
+    in_block = 4 * per_dev
     blocks = docs // in_block
     row = 0
     for block in range(blocks):
         for h in range(2):
             rows = pl.ds(h * half, half)
             for s in range(in_block):
-                entry = block * in_block + (s + h * per_dev) % in_block
+                entry = block * in_block + (s ^ (h * per_dev))
                 hit = (token_row == float(entry)).astype(F32).astype(BF16)
                 hit = jnp.concatenate([hit, hit], axis=1)
                 left[row:row + half, :2 * tokens] = pair_hi[rows, :] * hit
@@ -181,33 +185,47 @@
     any_spec = pl.BlockSpec(memory_space=pl.ANY)
     vmem = pl.BlockSpec(memory_space=pltpu.VMEM)
     half_shape = jax.ShapeDtypeStruct((rows // 2, LANES), F32)
-    keep, send = pl.pallas_call(
-        functools.partial(low_kernel, (bits, hop_bits, k_bit, per_dev, docs, og_chunk, hid_chunk)),
-        out_shape=(half_shape, half_shape),
-        in_specs=[any_spec] * 4 + [vmem],
+    low_shape = jax.ShapeDtypeStruct((rank, tokens), F32)
+    grad_low, input_low = pl.pallas_call(
+        functools.partial(low_kernel, og_chunk, hid_chunk),
+        out_shape=(low_shape, low_shape),
+        in_specs=[any_spec] * 4,
         out_specs=(vmem, vmem),
         scratch_shapes=[
             pltpu.VMEM((tokens, ff), BF16),
             pltpu.VMEM((tokens, d), BF16),
             pltpu.VMEM((rank, ff), BF16),
             pltpu.VMEM((rank, d), BF16),
-            pltpu.VMEM((rank // 2, 2 * tokens), BF16),
-            pltpu.VMEM((rank // 2, 2 * tokens), BF16),
-            pltpu.VMEM((rows, 4 * tokens), BF16),
             pltpu.SemaphoreType.DMA((2, d // og_chunk)),
             pltpu.SemaphoreType.DMA((2, ff // hid_chunk)),
         ],
-        compiler_params=pltpu.CompilerParams(vmem_limit_bytes=53 << 20),
+        compiler_params=pltpu.CompilerParams(vmem_limit_bytes=(53 << 20) + (1 << 19)),
         cost_estimate=pl.CostEstimate(
             flops=2 * tokens * rank * (ff + d),
             bytes_accessed=2 * (tokens + rank) * (ff + d),
             transcendentals=0,
         ),
         name="low",
-    )(hidden, out_grad, in_proj.T, out_proj.T, jnp.stack([doc_lengths, doc_slot]))
+    )(hidden, out_grad, in_proj.T, out_proj.T)
+    keep, send = pl.pallas_call(
+        functools.partial(outer_kernel, (hop_bits, k_bit, per_dev, docs)),
+        out_shape=(half_shape, half_shape),
+        in_specs=[vmem] * 4,
+        out_specs=(vmem, vmem),
+        scratch_shapes=[
+            pltpu.VMEM((rank // 2, 2 * tokens), BF16),
+            pltpu.VMEM((rank // 2, 2 * tokens), BF16),
+            pltpu.VMEM((rows, 4 * tokens), BF16),
+        ],
+        compiler_params=pltpu.CompilerParams(vmem_limit_bytes=32 << 20),
+        cost_estimate=pl.CostEstimate(
+            flops=2 * rows * 4 * tokens * 2 * LANES, bytes_accessed=1 << 20, transcendentals=0
+        ),
+        name="outer",
+    )(grad_low, input_low, doc_lengths.reshape(1, docs), doc_slot.reshape(1, docs))
 
     sums = []
-    for b in hop_bits:
+    for b in hop_bits[:-1] + (k_bit,):
         got = swap(send, b)
         size = keep.shape[0] // 2
         total = keep + got
@@ -225,7 +243,7 @@
             q, _ = lax.optimization_barrier((q, sums[0]))
         q_parts = (q, swap(q, b))
         q_bits = (b,) + q_bits
-    got = swap(send, k_bit)
+    got = swap(send, top)
 
     width = n * per_q
     terms = 8 * per_dev

time: 33.1 us -> 32.4 us (0.979)
  waiting for transfers between devices: 11.2 us -> 10.2 us
  starting transfers between devices: 13.4 us -> 14.2 us
  other arithmetic: 1.33 us -> 0.65 us
    ppermute x9, waiting for transfers between devices: 11.2 us -> 10.2 us  [swap(): return lax.ppermute(x, 'ctx', [(i, i ^ 1 << b) for i in range(n)])]
    ppermute x9, starting transfers between devices: 13.4 us -> 14.2 us  [swap(): return lax.ppermute(x, 'ctx', [(i, i ^ 1 << b) for i in range(n)])]
    another operation x1 -> x0, other arithmetic: 0.68 us -> none  [shards(): jnp.stack([doc_lengths, doc_slot])]
    pallas_call x1 -> x2, Pallas kernels: 6.17 us -> 6.25 us  [the longest x1 5.4 us: shards(): pl.pallas_call(functools.partial(low_kernel, og_chunk, hid_chunk), out_sh...]
  transfers between devices with their start and end apart: 9 -> 9, of which waited for: 4 -> 5; matrix products, arithmetic and copies ran while one was open for 3% -> 1% of each run, Pallas kernels for 20% -> 20%
where the time goes in v5:
time: 32.4 us; the launch traced here: 32.2 us
  starting transfers between devices  14.2 us (44%)
  waiting for transfers between devices  10.2 us (31%)
  Pallas kernels  6.89 us (21%)
  other arithmetic  0.65 us (2%)
    ppermute x9, starting transfers between devices, swap(): return lax.ppermute(x, 'ctx', [(i, i ^ 1 << b) for i in range(n)])  14.2 us
    ppermute x9, waiting for transfers between devices, swap(): return lax.ppermute(x, 'ctx', [(i, i ^ 1 << b) for i in range(n)])  10.2 us
    pallas_call x1, Pallas kernels, shards(): pl.pallas_call(functools.partial(low_kernel, og_chunk, hid_chunk), out_sh...  5.4 us
    pallas_call x1, Pallas kernels, shards(): pl.pallas_call(functools.partial(outer_kernel, (hop_bits, k_bit, per_dev,...  0.85 us
  transfers between devices with their start and end apart: 9, of which 5 were waited for; matrix products, arithmetic and copies ran while one was open for 1% of the time, Pallas kernels for 20%

profile of v5, /device:TPU:0, one launch (start us, length us, event | category | flops | bytes accessed | tf_op | source)
XLA Modules:
  0.0 32.2 jit_solution(1195996783405228805)
XLA Ops:
  0.0 4.0 %collective-permute-start.4 = (bf16[16,4096]{1,0:T(8,128)(2,1)}, bf16[16,4096]{1,0:T(8,128)(2,1)S(1)}, u32[]{:S(2)}, u32[]{:S(2)}) collective-permute-start(bf16[16,4096]{1,0:T(8,128)(2,1)} %param.13), channel_id=1, source_target_pairs={{0,8},{1,9},{2,10},{3,11},{4,12},{5,13},{6,14},{7,15},{8,0},{9,1},... | collective-permute-start | bytes 393224 | tf_op jit(solution)/shard_map/ppermute | solution.py:178
  4.0 0.0 copy-start
  4.0 0.0 copy-start.1
  4.0 0.0 copy-start.2
  4.0 5.4 %low.1 = (f32[64,256]{1,0:T(8,128)S(1)}, f32[64,256]{1,0:T(8,128)S(1)}) custom-call(bf16[256,14336]{1,0:T(8,128)(2,1)} %hid.1, bf16[256,4096]{1,0:T(8,128)(2,1)} %og.1, bf16[64,14336]{1,0:T(8,128)(2,1)} %bitcast.6, bf16[64,4096]{1,0:T(8,128)(2,1)} %bitcast.7), custom_call_target="tpu_custom_call" | custom-call | flops 603979776 | bytes 11796480 | tf_op jit(solution)/shard_map/low/pallas_call | solution.py:189
  9.5 0.0 copy-done
  9.5 0.0 copy-done.1
  9.5 0.8 %outer.1 = (f32[512,128]{1,0:T(8,128)S(1)}, f32[512,128]{1,0:T(8,128)S(1)}) custom-call(f32[64,256]{1,0:T(8,128)S(1)} %get-tuple-element.14.grad_low, f32[64,256]{1,0:T(8,128)S(1)} %get-tuple-element.15.input_low, s32[1,32]{1,0:T(1,128)S(1)} %bitcast.4, s32[1,32]{1,0:T(1,128)S(1)} %bitcast.5), custom_call_target="tpu_custom_call" | custom-call | flops 536870912 | bytes 1048576 | tf_op jit(solution)/shard_map/outer/pallas_call | solution.py:210
  10.3 0.1 collective-permute-start
  10.4 0.0 copy-done.2
  10.4 0.1 collective-permute-done.4
  10.6 1.6 %collective-permute-start.5 = (bf16[32,2048]{1,0:T(8,128)(2,1)S(1)}, bf16[32,2048]{1,0:T(8,128)(2,1)S(1)}, u32[]{:S(2)}, u32[]{:S(2)}) collective-permute-start(bf16[32,2048]{1,0:T(8,128)(2,1)S(1)} %get-tuple-element.24), channel_id=1, source_target_pairs={{0,4},{1,5},{2,6},{3,7},{4,0},{5,1},{6,2},{7,3},{8,12},{9,13},{10,... | collective-permute-start | bytes 393224 | tf_op jit(solution)/shard_map/ppermute | solution.py:178
  12.2 0.0 collective-permute-done
  12.2 1.6 %collective-permute-start.1 = (f32[256,128]{1,0:T(8,128)S(1)}, f32[256,128]{1,0:T(8,128)S(1)}, u32[]{:S(2)}, u32[]{:S(2)}) collective-permute-start(f32[256,128]{1,0:T(8,128)S(1)} %slice.25), channel_id=1, source_target_pairs={{0,2},{1,3},{2,0},{3,1},{4,6},{5,7},{6,4},{7,5},{8,10},{9,11},{10,... | collective-permute-start | bytes 393224 | tf_op jit(solution)/shard_map/ppermute | solution.py:178
  13.8 2.7 %collective-permute-done.5 = bf16[32,2048]{1,0:T(8,128)(2,1)S(1)} collective-permute-done((bf16[32,2048]{1,0:T(8,128)(2,1)S(1)}, bf16[32,2048]{1,0:T(8,128)(2,1)S(1)}, u32[]{:S(2)}, u32[]{:S(2)}) %collective-permute-start.5) | collective-permute-done | bytes 131104 | tf_op jit(solution)/shard_map/ppermute | solution.py:178
  16.5 1.6 %collective-permute-start.6 = (bf16[64,2048]{1,0:T(8,128)(2,1)S(1)}, bf16[64,2048]{1,0:T(8,128)(2,1)S(1)}, u32[]{:S(2)}, u32[]{:S(2)}) collective-permute-start(bf16[64,2048]{1,0:T(8,128)(2,1)S(1)} %pad_maximum_fusion), channel_id=1, source_target_pairs={{0,2},{1,3},{2,0},{3,1},{4,6},{5,7},{6,4},{7,5},{8,10},{9,11},{10,... | collective-permute-start | bytes 786440 | tf_op jit(solution)/shard_map/ppermute | solution.py:178
  18.1 0.0 collective-permute-done.1
  18.1 1.6 %collective-permute-start.2 = (f32[128,128]{1,0:T(8,128)S(1)}, f32[128,128]{1,0:T(8,128)S(1)}, u32[]{:S(2)}, u32[]{:S(2)}) collective-permute-start(f32[128,128]{1,0:T(8,128)S(1)} %slice.27), channel_id=1, source_target_pairs={{0,4},{1,5},{2,6},{3,7},{4,0},{5,1},{6,2},{7,3},{8,12},{9,13},{10,... | collective-permute-start | bytes 196616 | tf_op jit(solution)/shard_map/ppermute | solution.py:178
  19.8 2.7 %collective-permute-done.2 = f32[128,128]{1,0:T(8,128)S(1)} collective-permute-done((f32[128,128]{1,0:T(8,128)S(1)}, f32[128,128]{1,0:T(8,128)S(1)}, u32[]{:S(2)}, u32[]{:S(2)}) %collective-permute-start.2) | collective-permute-done | bytes 65568 | tf_op jit(solution)/shard_map/ppermute | solution.py:178
  22.5 2.1 %collective-permute-start.3 = (f32[64,128]{1,0:T(8,128)S(1)}, f32[64,128]{1,0:T(8,128)S(1)}, u32[]{:S(2)}, u32[]{:S(2)}) collective-permute-start(f32[64,128]{1,0:T(8,128)S(1)} %get-tuple-element.25), channel_id=1, source_target_pairs={{0,8},{1,9},{2,10},{3,11},{4,12},{5,13},{6,14},{7,15},{8,0},{9,1},... | collective-permute-start | bytes 98312 | tf_op jit(solution)/shard_map/ppermute | solution.py:178
  24.5 0.0 collective-permute-done.6
  24.5 0.1 collective-permute-start.7
  24.6 2.7 %collective-permute-done.3.grads_b = f32[64,128]{1,0:T(8,128)S(1)} collective-permute-done((f32[64,128]{1,0:T(8,128)S(1)}, f32[64,128]{1,0:T(8,128)S(1)}, u32[]{:S(2)}, u32[]{:S(2)}) %collective-permute-start.3) | collective-permute-done | bytes 32800 | tf_op jit(solution)/shard_map/ppermute | solution.py:178
  27.3 0.3 near_scores.1
  27.6 0.0 collective-permute-done.7.q_b
  27.7 0.3 %scores.1 = (f32[2,256]{1,0:T(2,128)S(1)}, f32[2,256]{1,0:T(2,128)S(1)}) custom-call(bf16[16,2048]{1,0:T(8,128)(2,1)S(1)} %get-tuple-element.19.left, f32[128,16]{1,0:T(8,128)S(1)} %get-tuple-element.20.out_a, bf16[128,2048]{1,0:T(8,128)(2,1)S(1)} %collective-permute-done.7.q_b), custom_call_target="tpu_custom_call" | custom-call | tf_op jit(solution)/shard_map/scores/pallas_call | solution.py:264
  28.0 1.6 %collective-permute-start.8 = (f32[2,256]{1,0:T(2,128)S(1)}, f32[2,256]{1,0:T(2,128)S(1)}, u32[]{:S(2)}, u32[]{:S(2)}) collective-permute-start(f32[2,256]{1,0:T(2,128)S(1)} %get-tuple-element.22), channel_id=1, source_target_pairs={{0,4},{1,5},{2,6},{3,7},{4,0},{5,1},{6,2},{7,3},{8,12},{9,13},{10,... | collective-permute-start | bytes 6152 | tf_op jit(solution)/shard_map/ppermute | solution.py:178
  29.6 2.0 %collective-permute-done.8 = f32[2,256]{1,0:T(2,128)S(1)} collective-permute-done((f32[2,256]{1,0:T(2,128)S(1)}, f32[2,256]{1,0:T(2,128)S(1)}, u32[]{:S(2)}, u32[]{:S(2)}) %collective-permute-start.8) | collective-permute-done | bytes 2080 | tf_op jit(solution)/shard_map/ppermute | solution.py:178
  31.6 0.6 %add.23 = f32[2,256]{1,0:T(2,128)} add(f32[2,256]{1,0:T(2,128)S(1)} %get-tuple-element.21, f32[2,256]{1,0:T(2,128)S(1)} %collective-permute-done.8) | non-fusion elementwise | flops 512 | bytes 6144 | tf_op jit(solution)/shard_map/add | solution.py:273
  (12 shorter events, 0.2 us)
Async XLA Ops:
  0.0 10.5 %collective-permute-start.4 = (bf16[16,4096]{1,0:T(8,128)(2,1)}, bf16[16,4096]{1,0:T(8,128)(2,1)S(1)}, u32[]{:S(2)}, u32[]{:S(2)}) collective-permute-start(bf16[16,4096]{1,0:T(8,128)(2,1)} %param.13), channel_id=1, source_target_pairs={{0,8},{1,9},{2,10},{3,11},{4,12},{5,13},{6,14},{7,15},{8,0},{9,1},... | collective-permute-start | bytes 393224 | tf_op jit(solution)/shard_map/ppermute | solution.py:178
  4.0 5.4 %copy-start = (s32[32]{0:T(128)S(1)}, s32[32]{0:T(128)}, u32[]{:S(2)}) copy-start(s32[32]{0:T(128)} %param.11) | copy-start | bytes 388
  4.0 5.4 %copy-start.1 = (s32[32]{0:T(128)S(1)}, s32[32]{0:T(128)}, u32[]{:S(2)}) copy-start(s32[32]{0:T(128)} %param.12) | copy-start | bytes 388
  4.0 6.4 %copy-start.2 = (bf16[16,4096]{1,0:T(8,128)(2,1)S(1)}, bf16[16,4096]{1,0:T(8,128)(2,1)}, u32[]{:S(2)}) copy-start(bf16[16,4096]{1,0:T(8,128)(2,1)} %param.13) | copy-start | bytes 393220
  10.3 1.8 %collective-permute-start = (f32[512,128]{1,0:T(8,128)S(1)}, f32[512,128]{1,0:T(8,128)S(1)}, u32[]{:S(2)}, u32[]{:S(2)}) collective-permute-start(f32[512,128]{1,0:T(8,128)S(1)} %get-tuple-element.17), channel_id=1, source_target_pairs={{0,1},{1,0},{2,3},{3,2},{4,5},{5,4},{6,7},{7,6},{8,9},{9,8},{10,11... | collective-permute-start | bytes 786440 | tf_op jit(solution)/shard_map/ppermute | solution.py:178
  10.6 5.9 %collective-permute-start.5 = (bf16[32,2048]{1,0:T(8,128)(2,1)S(1)}, bf16[32,2048]{1,0:T(8,128)(2,1)S(1)}, u32[]{:S(2)}, u32[]{:S(2)}) collective-permute-start(bf16[32,2048]{1,0:T(8,128)(2,1)S(1)} %get-tuple-element.24), channel_id=1, source_target_pairs={{0,4},{1,5},{2,6},{3,7},{4,0},{5,1},{6,2},{7,3},{8,12},{9,13},{10,... | collective-permute-start | bytes 393224 | tf_op jit(solution)/shard_map/ppermute | solution.py:178
  12.2 5.9 %collective-permute-start.1 = (f32[256,128]{1,0:T(8,128)S(1)}, f32[256,128]{1,0:T(8,128)S(1)}, u32[]{:S(2)}, u32[]{:S(2)}) collective-permute-start(f32[256,128]{1,0:T(8,128)S(1)} %slice.25), channel_id=1, source_target_pairs={{0,2},{1,3},{2,0},{3,1},{4,6},{5,7},{6,4},{7,5},{8,10},{9,11},{10,... | collective-permute-start | bytes 393224 | tf_op jit(solution)/shard_map/ppermute | solution.py:178
  16.5 8.0 %collective-permute-start.6 = (bf16[64,2048]{1,0:T(8,128)(2,1)S(1)}, bf16[64,2048]{1,0:T(8,128)(2,1)S(1)}, u32[]{:S(2)}, u32[]{:S(2)}) collective-permute-start(bf16[64,2048]{1,0:T(8,128)(2,1)S(1)} %pad_maximum_fusion), channel_id=1, source_target_pairs={{0,2},{1,3},{2,0},{3,1},{4,6},{5,7},{6,4},{7,5},{8,10},{9,11},{10,... | collective-permute-start | bytes 786440 | tf_op jit(solution)/shard_map/ppermute | solution.py:178
  18.1 4.3 %collective-permute-start.2 = (f32[128,128]{1,0:T(8,128)S(1)}, f32[128,128]{1,0:T(8,128)S(1)}, u32[]{:S(2)}, u32[]{:S(2)}) collective-permute-start(f32[128,128]{1,0:T(8,128)S(1)} %slice.27), channel_id=1, source_target_pairs={{0,4},{1,5},{2,6},{3,7},{4,0},{5,1},{6,2},{7,3},{8,12},{9,13},{10,... | collective-permute-start | bytes 196616 | tf_op jit(solution)/shard_map/ppermute | solution.py:178
  22.5 4.9 %collective-permute-start.3 = (f32[64,128]{1,0:T(8,128)S(1)}, f32[64,128]{1,0:T(8,128)S(1)}, u32[]{:S(2)}, u32[]{:S(2)}) collective-permute-start(f32[64,128]{1,0:T(8,128)S(1)} %get-tuple-element.25), channel_id=1, source_target_pairs={{0,8},{1,9},{2,10},{3,11},{4,12},{5,13},{6,14},{7,15},{8,0},{9,1},... | collective-permute-start | bytes 98312 | tf_op jit(solution)/shard_map/ppermute | solution.py:178
  24.5 3.1 %collective-permute-start.7 = (bf16[128,2048]{1,0:T(8,128)(2,1)S(1)}, bf16[128,2048]{1,0:T(8,128)(2,1)S(1)}, u32[]{:S(2)}, u32[]{:S(2)}) collective-permute-start(bf16[128,2048]{1,0:T(8,128)(2,1)S(1)} %constant_dynamic-update-slice_fusion.2.q), channel_id=1, source_target_pairs={{0,1},{1,0},{2,3},{3,2},{4,5},{5,4},{6,7},{7,6},{8,9},{9,8},{10,11... | collective-permute-start | bytes 1572872 | tf_op jit(solution)/shard_map/ppermute | solution.py:178
  28.0 3.6 %collective-permute-start.8 = (f32[2,256]{1,0:T(2,128)S(1)}, f32[2,256]{1,0:T(2,128)S(1)}, u32[]{:S(2)}, u32[]{:S(2)}) collective-permute-start(f32[2,256]{1,0:T(2,128)S(1)} %get-tuple-element.22), channel_id=1, source_target_pairs={{0,4},{1,5},{2,6},{3,7},{4,0},{5,1},{6,2},{7,3},{8,12},{9,13},{10,... | collective-permute-start | bytes 6152 | tf_op jit(solution)/shard_map/ppermute | solution.py:178

commit v6 on v5

--- a/solution.py
+++ b/solution.py
@@ -46,11 +46,10 @@
             for copy in copies:
                 copy.wait()
         (_, og_cols, _), (_, hid_cols, _) = fetched
-        start, size = hid_cols.start, hid_chunk // 2
-        parts = (
-            (og_v, w_out_v, og_cols),
-            (hid_v, w_in_v, pl.ds(start, size)),
-            (hid_v, w_in_v, pl.ds(pl.multiple_of(start + size, size), size)),
+        size = hid_chunk // 4
+        parts = ((og_v, w_out_v, og_cols),) + tuple(
+            (hid_v, w_in_v, pl.ds(pl.multiple_of(hid_cols.start + j * size, LANES), size))
+            for j in range(4)
         )
         return tuple(
             total + lax.dot_general(x[:, cols], w[:, cols], NT, preferred_element_type=F32)
@@ -58,8 +57,8 @@
         )
 
     zeros = jnp.zeros((tokens, rank), F32)
-    grad, first, second = lax.fori_loop(0, hid.shape[1] // hid_chunk, step, (zeros,) * 3)
-    grad_low[...], input_low[...] = grad.T, (first + second).T
+    grad, *inputs = lax.fori_loop(0, hid.shape[1] // hid_chunk, step, (zeros,) * 5)
+    grad_low[...], input_low[...] = grad.T, ((inputs[0] + inputs[1]) + (inputs[2] + inputs[3])).T
 
 
 def outer_kernel(
@@ -170,7 +169,7 @@
     docs = doc_slot.shape[0]
     per_dev = docs // n
     per_q = queries.shape[0]
-    k_bit, top = 2, bits - 1
+    k_bit, top = 1, bits - 1
     hop_bits = tuple(b for b in range(bits) if b != k_bit)
     me = lax.axis_index("ctx")
 

time: 32.4 us -> 32.4 us (level)
  no operation moved by 1% of the time
where the time goes in v6:
time: 32.4 us; the launch traced here: 32.3 us
  starting transfers between devices  14.3 us (44%)
  waiting for transfers between devices  10.1 us (31%)
  Pallas kernels  6.92 us (21%)
  other arithmetic  0.65 us (2%)
    ppermute x9, starting transfers between devices, swap(): return lax.ppermute(x, 'ctx', [(i, i ^ 1 << b) for i in range(n)])  14.3 us
    ppermute x9, waiting for transfers between devices, swap(): return lax.ppermute(x, 'ctx', [(i, i ^ 1 << b) for i in range(n)])  10.1 us
    pallas_call x1, Pallas kernels, shards(): pl.pallas_call(functools.partial(low_kernel, og_chunk, hid_chunk), out_sh...  5.43 us
    pallas_call x1, Pallas kernels, shards(): pl.pallas_call(functools.partial(outer_kernel, (hop_bits, k_bit, per_dev,...  0.86 us
  transfers between devices with their start and end apart: 9, of which 5 were waited for; matrix products, arithmetic and copies ran while one was open for 1% of the time, Pallas kernels for 20%

profile of v6, /device:TPU:0, one launch (start us, length us, event | category | flops | bytes accessed | tf_op | source)
XLA Modules:
  0.0 32.3 jit_solution(6326841674930369372)
XLA Ops:
  0.0 4.0 %collective-permute-start.4 = (bf16[16,4096]{1,0:T(8,128)(2,1)}, bf16[16,4096]{1,0:T(8,128)(2,1)S(1)}, u32[]{:S(2)}, u32[]{:S(2)}) collective-permute-start(bf16[16,4096]{1,0:T(8,128)(2,1)} %param.13), channel_id=1, source_target_pairs={{0,8},{1,9},{2,10},{3,11},{4,12},{5,13},{6,14},{7,15},{8,0},{9,1},... | collective-permute-start | bytes 393224 | tf_op jit(solution)/shard_map/ppermute | solution.py:177
  4.0 0.0 copy-start
  4.0 0.0 copy-start.1
  4.0 0.0 copy-start.2
  4.0 5.4 %low.1 = (f32[64,256]{1,0:T(8,128)S(1)}, f32[64,256]{1,0:T(8,128)S(1)}) custom-call(bf16[256,14336]{1,0:T(8,128)(2,1)} %hid.1, bf16[256,4096]{1,0:T(8,128)(2,1)} %og.1, bf16[64,14336]{1,0:T(8,128)(2,1)} %bitcast.6, bf16[64,4096]{1,0:T(8,128)(2,1)} %bitcast.7), custom_call_target="tpu_custom_call" | custom-call | flops 603979776 | bytes 11796480 | tf_op jit(solution)/shard_map/low/pallas_call | solution.py:188
  9.5 0.0 copy-done
  9.5 0.0 copy-done.1
  9.5 0.9 %outer.1 = (f32[512,128]{1,0:T(8,128)S(1)}, f32[512,128]{1,0:T(8,128)S(1)}) custom-call(f32[64,256]{1,0:T(8,128)S(1)} %get-tuple-element.14.grad_low, f32[64,256]{1,0:T(8,128)S(1)} %get-tuple-element.15.input_low, s32[1,32]{1,0:T(1,128)S(1)} %bitcast.4, s32[1,32]{1,0:T(1,128)S(1)} %bitcast.5), custom_call_target="tpu_custom_call" | custom-call | flops 536870912 | bytes 1048576 | tf_op jit(solution)/shard_map/outer/pallas_call | solution.py:209
  10.4 0.1 collective-permute-start
  10.4 0.0 copy-done.2
  10.5 0.1 collective-permute-done.4
  10.6 1.7 %collective-permute-start.5 = (bf16[32,2048]{1,0:T(8,128)(2,1)S(1)}, bf16[32,2048]{1,0:T(8,128)(2,1)S(1)}, u32[]{:S(2)}, u32[]{:S(2)}) collective-permute-start(bf16[32,2048]{1,0:T(8,128)(2,1)S(1)} %get-tuple-element.24), channel_id=1, source_target_pairs={{0,2},{1,3},{2,0},{3,1},{4,6},{5,7},{6,4},{7,5},{8,10},{9,11},{10,... | collective-permute-start | bytes 393224 | tf_op jit(solution)/shard_map/ppermute | solution.py:177
  12.3 0.0 collective-permute-done
  12.3 1.5 %collective-permute-start.1 = (f32[256,128]{1,0:T(8,128)S(1)}, f32[256,128]{1,0:T(8,128)S(1)}, u32[]{:S(2)}, u32[]{:S(2)}) collective-permute-start(f32[256,128]{1,0:T(8,128)S(1)} %slice.25), channel_id=1, source_target_pairs={{0,4},{1,5},{2,6},{3,7},{4,0},{5,1},{6,2},{7,3},{8,12},{9,13},{10,... | collective-permute-start | bytes 393224 | tf_op jit(solution)/shard_map/ppermute | solution.py:177
  13.8 2.7 %collective-permute-done.5 = bf16[32,2048]{1,0:T(8,128)(2,1)S(1)} collective-permute-done((bf16[32,2048]{1,0:T(8,128)(2,1)S(1)}, bf16[32,2048]{1,0:T(8,128)(2,1)S(1)}, u32[]{:S(2)}, u32[]{:S(2)}) %collective-permute-start.5) | collective-permute-done | bytes 131104 | tf_op jit(solution)/shard_map/ppermute | solution.py:177
  16.5 1.6 %collective-permute-start.6 = (bf16[64,2048]{1,0:T(8,128)(2,1)S(1)}, bf16[64,2048]{1,0:T(8,128)(2,1)S(1)}, u32[]{:S(2)}, u32[]{:S(2)}) collective-permute-start(bf16[64,2048]{1,0:T(8,128)(2,1)S(1)} %pad_maximum_fusion), channel_id=1, source_target_pairs={{0,4},{1,5},{2,6},{3,7},{4,0},{5,1},{6,2},{7,3},{8,12},{9,13},{10,... | collective-permute-start | bytes 786440 | tf_op jit(solution)/shard_map/ppermute | solution.py:177
  18.1 0.0 collective-permute-done.1
  18.2 1.6 %collective-permute-start.2 = (f32[128,128]{1,0:T(8,128)S(1)}, f32[128,128]{1,0:T(8,128)S(1)}, u32[]{:S(2)}, u32[]{:S(2)}) collective-permute-start(f32[128,128]{1,0:T(8,128)S(1)} %slice.27), channel_id=1, source_target_pairs={{0,2},{1,3},{2,0},{3,1},{4,6},{5,7},{6,4},{7,5},{8,10},{9,11},{10,... | collective-permute-start | bytes 196616 | tf_op jit(solution)/shard_map/ppermute | solution.py:177
  19.8 2.7 %collective-permute-done.2 = f32[128,128]{1,0:T(8,128)S(1)} collective-permute-done((f32[128,128]{1,0:T(8,128)S(1)}, f32[128,128]{1,0:T(8,128)S(1)}, u32[]{:S(2)}, u32[]{:S(2)}) %collective-permute-start.2) | collective-permute-done | bytes 65568 | tf_op jit(solution)/shard_map/ppermute | solution.py:177
  22.5 2.2 %collective-permute-start.3 = (f32[64,128]{1,0:T(8,128)S(1)}, f32[64,128]{1,0:T(8,128)S(1)}, u32[]{:S(2)}, u32[]{:S(2)}) collective-permute-start(f32[64,128]{1,0:T(8,128)S(1)} %get-tuple-element.25), channel_id=1, source_target_pairs={{0,8},{1,9},{2,10},{3,11},{4,12},{5,13},{6,14},{7,15},{8,0},{9,1},... | collective-permute-start | bytes 98312 | tf_op jit(solution)/shard_map/ppermute | solution.py:177
  24.7 0.0 collective-permute-done.6
  24.8 0.1 collective-permute-start.7
  24.8 2.6 %collective-permute-done.3.grads_b = f32[64,128]{1,0:T(8,128)S(1)} collective-permute-done((f32[64,128]{1,0:T(8,128)S(1)}, f32[64,128]{1,0:T(8,128)S(1)}, u32[]{:S(2)}, u32[]{:S(2)}) %collective-permute-start.3) | collective-permute-done | bytes 32800 | tf_op jit(solution)/shard_map/ppermute | solution.py:177
  27.4 0.3 near_scores.1
  27.7 0.0 collective-permute-done.7.q_b
  27.7 0.3 %scores.1 = (f32[2,256]{1,0:T(2,128)S(1)}, f32[2,256]{1,0:T(2,128)S(1)}) custom-call(bf16[16,2048]{1,0:T(8,128)(2,1)S(1)} %get-tuple-element.19.left, f32[128,16]{1,0:T(8,128)S(1)} %get-tuple-element.20.out_a, bf16[128,2048]{1,0:T(8,128)(2,1)S(1)} %collective-permute-done.7.q_b), custom_call_target="tpu_custom_call" | custom-call | tf_op jit(solution)/shard_map/scores/pallas_call | solution.py:263
  28.1 1.6 %collective-permute-start.8 = (f32[2,256]{1,0:T(2,128)S(1)}, f32[2,256]{1,0:T(2,128)S(1)}, u32[]{:S(2)}, u32[]{:S(2)}) collective-permute-start(f32[2,256]{1,0:T(2,128)S(1)} %get-tuple-element.22), channel_id=1, source_target_pairs={{0,2},{1,3},{2,0},{3,1},{4,6},{5,7},{6,4},{7,5},{8,10},{9,11},{10,... | collective-permute-start | bytes 6152 | tf_op jit(solution)/shard_map/ppermute | solution.py:177
  29.7 2.1 %collective-permute-done.8 = f32[2,256]{1,0:T(2,128)S(1)} collective-permute-done((f32[2,256]{1,0:T(2,128)S(1)}, f32[2,256]{1,0:T(2,128)S(1)}, u32[]{:S(2)}, u32[]{:S(2)}) %collective-permute-start.8) | collective-permute-done | bytes 2080 | tf_op jit(solution)/shard_map/ppermute | solution.py:177
  31.7 0.6 %add.23 = f32[2,256]{1,0:T(2,128)} add(f32[2,256]{1,0:T(2,128)S(1)} %get-tuple-element.21, f32[2,256]{1,0:T(2,128)S(1)} %collective-permute-done.8) | non-fusion elementwise | flops 512 | bytes 6144 | tf_op jit(solution)/shard_map/add | solution.py:272
  (12 shorter events, 0.2 us)
Async XLA Ops:
  0.0 10.5 %collective-permute-start.4 = (bf16[16,4096]{1,0:T(8,128)(2,1)}, bf16[16,4096]{1,0:T(8,128)(2,1)S(1)}, u32[]{:S(2)}, u32[]{:S(2)}) collective-permute-start(bf16[16,4096]{1,0:T(8,128)(2,1)} %param.13), channel_id=1, source_target_pairs={{0,8},{1,9},{2,10},{3,11},{4,12},{5,13},{6,14},{7,15},{8,0},{9,1},... | collective-permute-start | bytes 393224 | tf_op jit(solution)/shard_map/ppermute | solution.py:177
  4.0 5.4 %copy-start = (s32[32]{0:T(128)S(1)}, s32[32]{0:T(128)}, u32[]{:S(2)}) copy-start(s32[32]{0:T(128)} %param.11) | copy-start | bytes 388
  4.0 5.5 %copy-start.1 = (s32[32]{0:T(128)S(1)}, s32[32]{0:T(128)}, u32[]{:S(2)}) copy-start(s32[32]{0:T(128)} %param.12) | copy-start | bytes 388
  4.0 6.4 %copy-start.2 = (bf16[16,4096]{1,0:T(8,128)(2,1)S(1)}, bf16[16,4096]{1,0:T(8,128)(2,1)}, u32[]{:S(2)}) copy-start(bf16[16,4096]{1,0:T(8,128)(2,1)} %param.13) | copy-start | bytes 393220
  10.4 1.9 %collective-permute-start = (f32[512,128]{1,0:T(8,128)S(1)}, f32[512,128]{1,0:T(8,128)S(1)}, u32[]{:S(2)}, u32[]{:S(2)}) collective-permute-start(f32[512,128]{1,0:T(8,128)S(1)} %get-tuple-element.17), channel_id=1, source_target_pairs={{0,1},{1,0},{2,3},{3,2},{4,5},{5,4},{6,7},{7,6},{8,9},{9,8},{10,11... | collective-permute-start | bytes 786440 | tf_op jit(solution)/shard_map/ppermute | solution.py:177
  10.6 5.9 %collective-permute-start.5 = (bf16[32,2048]{1,0:T(8,128)(2,1)S(1)}, bf16[32,2048]{1,0:T(8,128)(2,1)S(1)}, u32[]{:S(2)}, u32[]{:S(2)}) collective-permute-start(bf16[32,2048]{1,0:T(8,128)(2,1)S(1)} %get-tuple-element.24), channel_id=1, source_target_pairs={{0,2},{1,3},{2,0},{3,1},{4,6},{5,7},{6,4},{7,5},{8,10},{9,11},{10,... | collective-permute-start | bytes 393224 | tf_op jit(solution)/shard_map/ppermute | solution.py:177
  12.3 5.8 %collective-permute-start.1 = (f32[256,128]{1,0:T(8,128)S(1)}, f32[256,128]{1,0:T(8,128)S(1)}, u32[]{:S(2)}, u32[]{:S(2)}) collective-permute-start(f32[256,128]{1,0:T(8,128)S(1)} %slice.25), channel_id=1, source_target_pairs={{0,4},{1,5},{2,6},{3,7},{4,0},{5,1},{6,2},{7,3},{8,12},{9,13},{10,... | collective-permute-start | bytes 393224 | tf_op jit(solution)/shard_map/ppermute | solution.py:177
  16.5 8.2 %collective-permute-start.6 = (bf16[64,2048]{1,0:T(8,128)(2,1)S(1)}, bf16[64,2048]{1,0:T(8,128)(2,1)S(1)}, u32[]{:S(2)}, u32[]{:S(2)}) collective-permute-start(bf16[64,2048]{1,0:T(8,128)(2,1)S(1)} %pad_maximum_fusion), channel_id=1, source_target_pairs={{0,4},{1,5},{2,6},{3,7},{4,0},{5,1},{6,2},{7,3},{8,12},{9,13},{10,... | collective-permute-start | bytes 786440 | tf_op jit(solution)/shard_map/ppermute | solution.py:177
  18.2 4.3 %collective-permute-start.2 = (f32[128,128]{1,0:T(8,128)S(1)}, f32[128,128]{1,0:T(8,128)S(1)}, u32[]{:S(2)}, u32[]{:S(2)}) collective-permute-start(f32[128,128]{1,0:T(8,128)S(1)} %slice.27), channel_id=1, source_target_pairs={{0,2},{1,3},{2,0},{3,1},{4,6},{5,7},{6,4},{7,5},{8,10},{9,11},{10,... | collective-permute-start | bytes 196616 | tf_op jit(solution)/shard_map/ppermute | solution.py:177
  22.5 4.9 %collective-permute-start.3 = (f32[64,128]{1,0:T(8,128)S(1)}, f32[64,128]{1,0:T(8,128)S(1)}, u32[]{:S(2)}, u32[]{:S(2)}) collective-permute-start(f32[64,128]{1,0:T(8,128)S(1)} %get-tuple-element.25), channel_id=1, source_target_pairs={{0,8},{1,9},{2,10},{3,11},{4,12},{5,13},{6,14},{7,15},{8,0},{9,1},... | collective-permute-start | bytes 98312 | tf_op jit(solution)/shard_map/ppermute | solution.py:177
  24.8 3.0 %collective-permute-start.7 = (bf16[128,2048]{1,0:T(8,128)(2,1)S(1)}, bf16[128,2048]{1,0:T(8,128)(2,1)S(1)}, u32[]{:S(2)}, u32[]{:S(2)}) collective-permute-start(bf16[128,2048]{1,0:T(8,128)(2,1)S(1)} %constant_dynamic-update-slice_fusion.2.q), channel_id=1, source_target_pairs={{0,1},{1,0},{2,3},{3,2},{4,5},{5,4},{6,7},{7,6},{8,9},{9,8},{10,11... | collective-permute-start | bytes 1572872 | tf_op jit(solution)/shard_map/ppermute | solution.py:177
  28.1 3.6 %collective-permute-start.8 = (f32[2,256]{1,0:T(2,128)S(1)}, f32[2,256]{1,0:T(2,128)S(1)}, u32[]{:S(2)}, u32[]{:S(2)}) collective-permute-start(f32[2,256]{1,0:T(2,128)S(1)} %get-tuple-element.22), channel_id=1, source_target_pairs={{0,2},{1,3},{2,0},{3,1},{4,6},{5,7},{6,4},{7,5},{8,10},{9,11},{10,... | collective-permute-start | bytes 6152 | tf_op jit(solution)/shard_map/ppermute | solution.py:177

commit v7 on v5

--- a/solution.py
+++ b/solution.py
@@ -63,7 +63,7 @@
 
 
 def outer_kernel(
-    plan, grad_low, input_low, lengths, slots, keep, send, pair_hi, pair_lo, left
+    plan, part, grad_low, input_low, lengths, slots, out, pair_hi, pair_lo, left
 ):
     hop_bits, k_bit, per_dev, docs = plan
     rank, tokens = grad_low.shape
@@ -112,9 +112,9 @@
     right = jnp.concatenate([right, right], axis=1)
 
     in_block = 4 * per_dev
-    blocks = docs // in_block
+    blocks = docs // in_block // 2
     row = 0
-    for block in range(blocks):
+    for block in range(part * blocks, (part + 1) * blocks):
         for h in range(2):
             rows = pl.ds(h * half, half)
             for s in range(in_block):
@@ -124,11 +124,8 @@
                 left[row:row + half, :2 * tokens] = pair_hi[rows, :] * hit
                 left[row:row + half, 2 * tokens:] = pair_lo[rows, :] * hit
                 row += half
-    size = keep.shape[0]
-    for part, out_ref in enumerate((send, keep)):
-        rows = left[(1 - part) * size:(2 - part) * size, :]
-        both = lax.dot_general(rows, right, NT, preferred_element_type=F32)
-        out_ref[...] = both[:, :LANES] + both[:, LANES:]
+    both = lax.dot_general(left[...], right, NT, preferred_element_type=F32)
+    out[...] = both[:, :LANES] + both[:, LANES:]
 
 
 def near_kernel(per_dev, grads_a, grads_b, q, left, out, total):
@@ -207,22 +204,25 @@
         ),
         name="low",
     )(hidden, out_grad, in_proj.T, out_proj.T)
-    keep, send = pl.pallas_call(
-        functools.partial(outer_kernel, (hop_bits, k_bit, per_dev, docs)),
-        out_shape=(half_shape, half_shape),
-        in_specs=[vmem] * 4,
-        out_specs=(vmem, vmem),
-        scratch_shapes=[
-            pltpu.VMEM((rank // 2, 2 * tokens), BF16),
-            pltpu.VMEM((rank // 2, 2 * tokens), BF16),
-            pltpu.VMEM((rows, 4 * tokens), BF16),
-        ],
-        compiler_params=pltpu.CompilerParams(vmem_limit_bytes=32 << 20),
-        cost_estimate=pl.CostEstimate(
-            flops=2 * rows * 4 * tokens * 2 * LANES, bytes_accessed=1 << 20, transcendentals=0
-        ),
-        name="outer",
-    )(grad_low, input_low, doc_lengths.reshape(1, docs), doc_slot.reshape(1, docs))
+    keep, send = [
+        pl.pallas_call(
+            functools.partial(outer_kernel, (hop_bits, k_bit, per_dev, docs), part),
+            out_shape=half_shape,
+            in_specs=[vmem] * 4,
+            out_specs=vmem,
+            scratch_shapes=[
+                pltpu.VMEM((rank // 2, 2 * tokens), BF16),
+                pltpu.VMEM((rank // 2, 2 * tokens), BF16),
+                pltpu.VMEM((rows // 2, 4 * tokens), BF16),
+            ],
+            compiler_params=pltpu.CompilerParams(vmem_limit_bytes=32 << 20),
+            cost_estimate=pl.CostEstimate(
+                flops=2 * rows * 4 * tokens * LANES, bytes_accessed=1 << 20, transcendentals=0
+            ),
+            name=name,
+        )(grad_low, input_low, doc_lengths.reshape(1, docs), doc_slot.reshape(1, docs))
+        for part, name in enumerate(("outer_keep", "outer_send"))
+    ]
 
     sums = []
     for b in hop_bits[:-1] + (k_bit,):

time: 32.4 us -> 32.5 us (level)
  starting transfers between devices: 14.2 us -> 13.6 us
  waiting for transfers between devices: 10.2 us -> 10.6 us
    ppermute x9, starting transfers between devices: 14.2 us -> 13.6 us  [swap(): return lax.ppermute(x, 'ctx', [(i, i ^ 1 << b) for i in range(n)])]
    ppermute x9, waiting for transfers between devices: 10.2 us -> 10.6 us  [swap(): return lax.ppermute(x, 'ctx', [(i, i ^ 1 << b) for i in range(n)])]
    pallas_call x1 -> x2, Pallas kernels: 0.85 us -> 1.13 us  [shards(): pl.pallas_call(functools.partial(outer_kernel, (hop_bits, k_bit, per_dev,...]
  transfers between devices with their start and end apart: 9 -> 9, of which waited for: 5 -> 6; matrix products, arithmetic and copies ran while one was open for 1% -> 1% of each run, Pallas kernels for 20% -> 21%
where the time goes in v7:
time: 32.5 us; the launch traced here: 32.3 us
  starting transfers between devices  13.6 us (42%)
  waiting for transfers between devices  10.6 us (33%)
  Pallas kernels  7.17 us (22%)
  other arithmetic  0.65 us (2%)
    ppermute x9, starting transfers between devices, swap(): return lax.ppermute(x, 'ctx', [(i, i ^ 1 << b) for i in range(n)])  13.6 us
    ppermute x9, waiting for transfers between devices, swap(): return lax.ppermute(x, 'ctx', [(i, i ^ 1 << b) for i in range(n)])  10.6 us
    pallas_call x1, Pallas kernels, shards(): pl.pallas_call(functools.partial(low_kernel, og_chunk, hid_chunk), out_sh...  5.4 us
    pallas_call x2, Pallas kernels, shards(): pl.pallas_call(functools.partial(outer_kernel, (hop_bits, k_bit, per_dev,...  1.13 us
  transfers between devices with their start and end apart: 9, of which 6 were waited for; matrix products, arithmetic and copies ran while one was open for 1% of the time, Pallas kernels for 21%

profile of v7, /device:TPU:0, one launch (start us, length us, event | category | flops | bytes accessed | tf_op | source)
XLA Modules:
  0.0 32.3 jit_solution(13527629050280580878)
XLA Ops:
  0.0 4.0 %collective-permute-start.4 = (bf16[16,4096]{1,0:T(8,128)(2,1)}, bf16[16,4096]{1,0:T(8,128)(2,1)S(1)}, u32[]{:S(2)}, u32[]{:S(2)}) collective-permute-start(bf16[16,4096]{1,0:T(8,128)(2,1)} %param.13), channel_id=1, source_target_pairs={{0,8},{1,9},{2,10},{3,11},{4,12},{5,13},{6,14},{7,15},{8,0},{9,1},... | collective-permute-start | bytes 393224 | tf_op jit(solution)/shard_map/ppermute | solution.py:175
  4.0 0.0 copy-start
  4.0 0.0 copy-start.1
  4.0 0.0 copy-start.2
  4.0 5.4 %low.1 = (f32[64,256]{1,0:T(8,128)S(1)}, f32[64,256]{1,0:T(8,128)S(1)}) custom-call(bf16[256,14336]{1,0:T(8,128)(2,1)} %hid.1, bf16[256,4096]{1,0:T(8,128)(2,1)} %og.1, bf16[64,14336]{1,0:T(8,128)(2,1)} %bitcast.8, bf16[64,4096]{1,0:T(8,128)(2,1)} %bitcast.9), custom_call_target="tpu_custom_call" | custom-call | flops 603979776 | bytes 11796480 | tf_op jit(solution)/shard_map/low/pallas_call | solution.py:186
  9.5 0.0 copy-done
  9.5 0.0 copy-done.1
  9.5 0.6 %outer_send.1 = f32[512,128]{1,0:T(8,128)S(1)} custom-call(f32[64,256]{1,0:T(8,128)S(1)} %get-tuple-element.12.grad_low, f32[64,256]{1,0:T(8,128)S(1)} %get-tuple-element.13.input_low, s32[1,32]{1,0:T(1,128)S(1)} %bitcast.4, s32[1,32]{1,0:T(1,128)S(1)} %bitcast.6), custom_call_target="tpu_custom_call" | custom-call | flops 268435456 | bytes 1048576 | tf_op jit(solution)/shard_map/outer_send/pallas_call | solution.py:208
  10.0 0.1 collective-permute-start
  10.1 0.0 copy-done.2
  10.2 0.4 %collective-permute-done.4 = bf16[16,4096]{1,0:T(8,128)(2,1)S(1)} collective-permute-done((bf16[16,4096]{1,0:T(8,128)(2,1)}, bf16[16,4096]{1,0:T(8,128)(2,1)S(1)}, u32[]{:S(2)}, u32[]{:S(2)}) %collective-permute-start.4) | collective-permute-done | bytes 131104 | tf_op jit(solution)/shard_map/ppermute | solution.py:175
  10.6 1.3 %collective-permute-start.5 = (bf16[32,2048]{1,0:T(8,128)(2,1)S(1)}, bf16[32,2048]{1,0:T(8,128)(2,1)S(1)}, u32[]{:S(2)}, u32[]{:S(2)}) collective-permute-start(bf16[32,2048]{1,0:T(8,128)(2,1)S(1)} %get-tuple-element.20), channel_id=1, source_target_pairs={{0,4},{1,5},{2,6},{3,7},{4,0},{5,1},{6,2},{7,3},{8,12},{9,13},{10,... | collective-permute-start | bytes 393224 | tf_op jit(solution)/shard_map/ppermute | solution.py:175
  11.9 0.6 %outer_keep.1 = f32[512,128]{1,0:T(8,128)S(1)} custom-call(f32[64,256]{1,0:T(8,128)S(1)} %get-tuple-element.12.grad_low, f32[64,256]{1,0:T(8,128)S(1)} %get-tuple-element.13.input_low, s32[1,32]{1,0:T(1,128)S(1)} %bitcast.5, s32[1,32]{1,0:T(1,128)S(1)} %bitcast.7), custom_call_target="tpu_custom_call" | custom-call | flops 268435456 | bytes 1048576 | tf_op jit(solution)/shard_map/outer_keep/pallas_call | solution.py:208
  12.4 0.0 collective-permute-done
  12.5 1.6 %collective-permute-start.1 = (f32[256,128]{1,0:T(8,128)S(1)}, f32[256,128]{1,0:T(8,128)S(1)}, u32[]{:S(2)}, u32[]{:S(2)}) collective-permute-start(f32[256,128]{1,0:T(8,128)S(1)} %slice.25), channel_id=1, source_target_pairs={{0,2},{1,3},{2,0},{3,1},{4,6},{5,7},{6,4},{7,5},{8,10},{9,11},{10,... | collective-permute-start | bytes 393224 | tf_op jit(solution)/shard_map/ppermute | solution.py:175
  14.1 2.1 %collective-permute-done.5 = bf16[32,2048]{1,0:T(8,128)(2,1)S(1)} collective-permute-done((bf16[32,2048]{1,0:T(8,128)(2,1)S(1)}, bf16[32,2048]{1,0:T(8,128)(2,1)S(1)}, u32[]{:S(2)}, u32[]{:S(2)}) %collective-permute-start.5) | collective-permute-done | bytes 131104 | tf_op jit(solution)/shard_map/ppermute | solution.py:175
  16.2 1.6 %collective-permute-start.6 = (bf16[64,2048]{1,0:T(8,128)(2,1)S(1)}, bf16[64,2048]{1,0:T(8,128)(2,1)S(1)}, u32[]{:S(2)}, u32[]{:S(2)}) collective-permute-start(bf16[64,2048]{1,0:T(8,128)(2,1)S(1)} %pad_maximum_fusion), channel_id=1, source_target_pairs={{0,2},{1,3},{2,0},{3,1},{4,6},{5,7},{6,4},{7,5},{8,10},{9,11},{10,... | collective-permute-start | bytes 786440 | tf_op jit(solution)/shard_map/ppermute | solution.py:175
  17.8 0.4 %collective-permute-done.1 = f32[256,128]{1,0:T(8,128)S(1)} collective-permute-done((f32[256,128]{1,0:T(8,128)S(1)}, f32[256,128]{1,0:T(8,128)S(1)}, u32[]{:S(2)}, u32[]{:S(2)}) %collective-permute-start.1) | collective-permute-done | bytes 131104 | tf_op jit(solution)/shard_map/ppermute | solution.py:175
  18.2 1.2 %collective-permute-start.2 = (f32[128,128]{1,0:T(8,128)S(1)}, f32[128,128]{1,0:T(8,128)S(1)}, u32[]{:S(2)}, u32[]{:S(2)}) collective-permute-start(f32[128,128]{1,0:T(8,128)S(1)} %slice.27), channel_id=1, source_target_pairs={{0,4},{1,5},{2,6},{3,7},{4,0},{5,1},{6,2},{7,3},{8,12},{9,13},{10,... | collective-permute-start | bytes 196616 | tf_op jit(solution)/shard_map/ppermute | solution.py:175
  19.5 3.1 %collective-permute-done.2 = f32[128,128]{1,0:T(8,128)S(1)} collective-permute-done((f32[128,128]{1,0:T(8,128)S(1)}, f32[128,128]{1,0:T(8,128)S(1)}, u32[]{:S(2)}, u32[]{:S(2)}) %collective-permute-start.2) | collective-permute-done | bytes 65568 | tf_op jit(solution)/shard_map/ppermute | solution.py:175
  22.6 2.5 %collective-permute-start.3 = (f32[64,128]{1,0:T(8,128)S(1)}, f32[64,128]{1,0:T(8,128)S(1)}, u32[]{:S(2)}, u32[]{:S(2)}) collective-permute-start(f32[64,128]{1,0:T(8,128)S(1)} %get-tuple-element.21), channel_id=1, source_target_pairs={{0,8},{1,9},{2,10},{3,11},{4,12},{5,13},{6,14},{7,15},{8,0},{9,1},... | collective-permute-start | bytes 98312 | tf_op jit(solution)/shard_map/ppermute | solution.py:175
  25.1 0.0 collective-permute-done.6
  25.1 0.1 collective-permute-start.7
  25.2 2.3 %collective-permute-done.3.grads_b = f32[64,128]{1,0:T(8,128)S(1)} collective-permute-done((f32[64,128]{1,0:T(8,128)S(1)}, f32[64,128]{1,0:T(8,128)S(1)}, u32[]{:S(2)}, u32[]{:S(2)}) %collective-permute-start.3) | collective-permute-done | bytes 32800 | tf_op jit(solution)/shard_map/ppermute | solution.py:175
  27.5 0.3 near_scores.1
  27.8 0.0 collective-permute-done.7.q_b
  27.8 0.3 %scores.1 = (f32[2,256]{1,0:T(2,128)S(1)}, f32[2,256]{1,0:T(2,128)S(1)}) custom-call(bf16[16,2048]{1,0:T(8,128)(2,1)S(1)} %get-tuple-element.15.left, f32[128,16]{1,0:T(8,128)S(1)} %get-tuple-element.16.out_a, bf16[128,2048]{1,0:T(8,128)(2,1)S(1)} %collective-permute-done.7.q_b), custom_call_target="tpu_custom_call" | custom-call | tf_op jit(solution)/shard_map/scores/pallas_call | solution.py:264
  28.1 1.2 %collective-permute-start.8 = (f32[2,256]{1,0:T(2,128)S(1)}, f32[2,256]{1,0:T(2,128)S(1)}, u32[]{:S(2)}, u32[]{:S(2)}) collective-permute-start(f32[2,256]{1,0:T(2,128)S(1)} %get-tuple-element.18), channel_id=1, source_target_pairs={{0,4},{1,5},{2,6},{3,7},{4,0},{5,1},{6,2},{7,3},{8,12},{9,13},{10,... | collective-permute-start | bytes 6152 | tf_op jit(solution)/shard_map/ppermute | solution.py:175
  29.4 2.4 %collective-permute-done.8 = f32[2,256]{1,0:T(2,128)S(1)} collective-permute-done((f32[2,256]{1,0:T(2,128)S(1)}, f32[2,256]{1,0:T(2,128)S(1)}, u32[]{:S(2)}, u32[]{:S(2)}) %collective-permute-start.8) | collective-permute-done | bytes 2080 | tf_op jit(solution)/shard_map/ppermute | solution.py:175
  31.7 0.6 %add.23 = f32[2,256]{1,0:T(2,128)} add(f32[2,256]{1,0:T(2,128)S(1)} %get-tuple-element.17, f32[2,256]{1,0:T(2,128)S(1)} %collective-permute-done.8) | non-fusion elementwise | flops 512 | bytes 6144 | tf_op jit(solution)/shard_map/add | solution.py:273
  (12 shorter events, 0.2 us)
Async XLA Ops:
  0.0 10.5 %collective-permute-start.4 = (bf16[16,4096]{1,0:T(8,128)(2,1)}, bf16[16,4096]{1,0:T(8,128)(2,1)S(1)}, u32[]{:S(2)}, u32[]{:S(2)}) collective-permute-start(bf16[16,4096]{1,0:T(8,128)(2,1)} %param.13), channel_id=1, source_target_pairs={{0,8},{1,9},{2,10},{3,11},{4,12},{5,13},{6,14},{7,15},{8,0},{9,1},... | collective-permute-start | bytes 393224 | tf_op jit(solution)/shard_map/ppermute | solution.py:175
  4.0 5.4 %copy-start = (s32[32]{0:T(128)S(1)}, s32[32]{0:T(128)}, u32[]{:S(2)}) copy-start(s32[32]{0:T(128)} %param.11) | copy-start | bytes 388
  4.0 5.4 %copy-start.1 = (s32[32]{0:T(128)S(1)}, s32[32]{0:T(128)}, u32[]{:S(2)}) copy-start(s32[32]{0:T(128)} %param.12) | copy-start | bytes 388
  4.0 6.1 %copy-start.2 = (bf16[16,4096]{1,0:T(8,128)(2,1)S(1)}, bf16[16,4096]{1,0:T(8,128)(2,1)}, u32[]{:S(2)}) copy-start(bf16[16,4096]{1,0:T(8,128)(2,1)} %param.13) | copy-start | bytes 393220
  10.0 2.4 %collective-permute-start = (f32[512,128]{1,0:T(8,128)S(1)}, f32[512,128]{1,0:T(8,128)S(1)}, u32[]{:S(2)}, u32[]{:S(2)}) collective-permute-start(f32[512,128]{1,0:T(8,128)S(1)} %outer_send.1), channel_id=1, source_target_pairs={{0,1},{1,0},{2,3},{3,2},{4,5},{5,4},{6,7},{7,6},{8,9},{9,8},{10,11... | collective-permute-start | bytes 786440 | tf_op jit(solution)/shard_map/ppermute | solution.py:175
  10.6 5.6 %collective-permute-start.5 = (bf16[32,2048]{1,0:T(8,128)(2,1)S(1)}, bf16[32,2048]{1,0:T(8,128)(2,1)S(1)}, u32[]{:S(2)}, u32[]{:S(2)}) collective-permute-start(bf16[32,2048]{1,0:T(8,128)(2,1)S(1)} %get-tuple-element.20), channel_id=1, source_target_pairs={{0,4},{1,5},{2,6},{3,7},{4,0},{5,1},{6,2},{7,3},{8,12},{9,13},{10,... | collective-permute-start | bytes 393224 | tf_op jit(solution)/shard_map/ppermute | solution.py:175
  12.5 5.7 %collective-permute-start.1 = (f32[256,128]{1,0:T(8,128)S(1)}, f32[256,128]{1,0:T(8,128)S(1)}, u32[]{:S(2)}, u32[]{:S(2)}) collective-permute-start(f32[256,128]{1,0:T(8,128)S(1)} %slice.25), channel_id=1, source_target_pairs={{0,2},{1,3},{2,0},{3,1},{4,6},{5,7},{6,4},{7,5},{8,10},{9,11},{10,... | collective-permute-start | bytes 393224 | tf_op jit(solution)/shard_map/ppermute | solution.py:175
  16.2 8.9 %collective-permute-start.6 = (bf16[64,2048]{1,0:T(8,128)(2,1)S(1)}, bf16[64,2048]{1,0:T(8,128)(2,1)S(1)}, u32[]{:S(2)}, u32[]{:S(2)}) collective-permute-start(bf16[64,2048]{1,0:T(8,128)(2,1)S(1)} %pad_maximum_fusion), channel_id=1, source_target_pairs={{0,2},{1,3},{2,0},{3,1},{4,6},{5,7},{6,4},{7,5},{8,10},{9,11},{10,... | collective-permute-start | bytes 786440 | tf_op jit(solution)/shard_map/ppermute | solution.py:175
  18.2 4.3 %collective-permute-start.2 = (f32[128,128]{1,0:T(8,128)S(1)}, f32[128,128]{1,0:T(8,128)S(1)}, u32[]{:S(2)}, u32[]{:S(2)}) collective-permute-start(f32[128,128]{1,0:T(8,128)S(1)} %slice.27), channel_id=1, source_target_pairs={{0,4},{1,5},{2,6},{3,7},{4,0},{5,1},{6,2},{7,3},{8,12},{9,13},{10,... | collective-permute-start | bytes 196616 | tf_op jit(solution)/shard_map/ppermute | solution.py:175
  22.6 4.9 %collective-permute-start.3 = (f32[64,128]{1,0:T(8,128)S(1)}, f32[64,128]{1,0:T(8,128)S(1)}, u32[]{:S(2)}, u32[]{:S(2)}) collective-permute-start(f32[64,128]{1,0:T(8,128)S(1)} %get-tuple-element.21), channel_id=1, source_target_pairs={{0,8},{1,9},{2,10},{3,11},{4,12},{5,13},{6,14},{7,15},{8,0},{9,1},... | collective-permute-start | bytes 98312 | tf_op jit(solution)/shard_map/ppermute | solution.py:175
  25.1 2.7 %collective-permute-start.7 = (bf16[128,2048]{1,0:T(8,128)(2,1)S(1)}, bf16[128,2048]{1,0:T(8,128)(2,1)S(1)}, u32[]{:S(2)}, u32[]{:S(2)}) collective-permute-start(bf16[128,2048]{1,0:T(8,128)(2,1)S(1)} %constant_dynamic-update-slice_fusion.2.q), channel_id=1, source_target_pairs={{0,1},{1,0},{2,3},{3,2},{4,5},{5,4},{6,7},{7,6},{8,9},{9,8},{10,11... | collective-permute-start | bytes 1572872 | tf_op jit(solution)/shard_map/ppermute | solution.py:175
  28.1 3.6 %collective-permute-start.8 = (f32[2,256]{1,0:T(2,128)S(1)}, f32[2,256]{1,0:T(2,128)S(1)}, u32[]{:S(2)}, u32[]{:S(2)}) collective-permute-start(f32[2,256]{1,0:T(2,128)S(1)} %get-tuple-element.18), channel_id=1, source_target_pairs={{0,4},{1,5},{2,6},{3,7},{4,0},{5,1},{6,2},{7,3},{8,12},{9,13},{10,... | collective-permute-start | bytes 6152 | tf_op jit(solution)/shard_map/ppermute | solution.py:175
